TPU v7x, 256 devices: a whole 4x4x8 slice. The times are simulated.
256 devices in a mesh: dp: 8 (over x, core), tensor: 32 (over y, z).
Axes of the slice: x: 4, y: 4, z: 8, core: 2. Of those that a mesh axis runs over, the one named last changes fastest.
Arguments:
- tokens: bfloat16 [4096, 4096], P(('dp', 'tensor')), may hold values from -6 to 6
- cotangent: bfloat16 [4096, 4096], P(('dp', 'tensor')), may hold values from -12 to 12
- loss_mask: int32 [4096], P(('dp', 'tensor')), may hold values from 0 to 1, as said below
- gate_weight: bfloat16 [4096, 14336], P(None, 'tensor'), may hold values from -0.09375 to 0.09375
- up_weight: bfloat16 [4096, 14336], P(None, 'tensor'), may hold values from -0.09375 to 0.09375
- down_weight: bfloat16 [14336, 4096], P('tensor'), may hold values from -0.046875 to 0.046875
- probe_seed: int32 [1], replicated, may hold values from 0 to 1048575
Outputs:
- diag_gate: float32 [4096, 14336], P('dp', 'tensor')
Inputs may be any that keep to these rules, and one draw needn't show every extreme that they name: `loss_mask`: 0 or 1; the first entry is 1.
All inputs are finite; a program needn't handle non-finite values.
Results may differ from a plain program's by a relative error of at most 0.0029.
Values may be sent and summed in bfloat16 or wider, within the bound.
A program may use at most 128 MiB of HBM per device.

v0:
```python
import jax
import jax.numpy as jnp
from jax import lax
from jax.sharding import PartitionSpec as P

FF = 14336


contract_rows = (((0,), (0,)), ((), ()))
contract_last = (((1,), (1,)), ((), ()))


def probe_signs(seed_value, row_count, col_count, first_col, full_width):
    row_index = lax.broadcasted_iota(jnp.int32, (row_count, col_count), 0)
    col_index = lax.broadcasted_iota(jnp.int32, (row_count, col_count), 1) + first_col
    hashed = (row_index * full_width + col_index) * jnp.int32(-1640531535) + seed_value * jnp.int32(
        668265263
    )
    hashed = hashed ^ lax.shift_right_logical(hashed, jnp.full_like(hashed, 15))
    hashed = hashed * jnp.int32(739982445)
    hashed = hashed ^ lax.shift_right_logical(hashed, jnp.full_like(hashed, 12))
    hashed = hashed * jnp.int32(695872825)
    hashed = hashed ^ lax.shift_right_logical(hashed, jnp.full_like(hashed, 15))
    lowbit = lax.shift_right_logical(hashed, jnp.full_like(hashed, 16)) & jnp.int32(1)
    return jnp.int32(1) - jnp.int32(2) * lowbit


def curvature(gate_pre):
    sigmoid_val = jax.nn.sigmoid(gate_pre)
    return sigmoid_val * (1.0 - sigmoid_val) * (2.0 + gate_pre * (1.0 - 2.0 * sigmoid_val))


def per_device(tokens, cotangent, loss_mask, gate_weight, up_weight, down_weight, probe_seed):
    width_dev = gate_weight.shape[1]
    feature_count = gate_weight.shape[0]
    out_rows = feature_count // lax.axis_size("dp")
    sign_table = probe_signs(
        probe_seed[0], feature_count, width_dev, lax.axis_index("tensor") * width_dev, FF
    )
    probe_bf = sign_table.astype(jnp.bfloat16)
    live_flags = loss_mask.astype(jnp.bfloat16)
    masked = cotangent * live_flags[:, None]
    features = lax.all_gather(tokens, "tensor", axis=0, tiled=True)
    masked_rows = lax.all_gather(masked, "tensor", axis=0, tiled=True)
    live_count = lax.psum(jnp.sum(live_flags.astype(jnp.float32)), ("dp", "tensor"))
    gate_pre = jnp.dot(features, gate_weight, preferred_element_type=jnp.float32)
    up_proj = jnp.dot(features, up_weight, preferred_element_type=jnp.float32)
    tangent = jnp.dot(features, probe_bf, preferred_element_type=jnp.float32)
    back_grad = lax.dot_general(
        masked_rows, down_weight, contract_last, preferred_element_type=jnp.float32
    )
    operand = (back_grad * up_proj * curvature(gate_pre) * tangent).astype(jnp.bfloat16)
    hessian = lax.psum_scatter(
        lax.dot_general(features, operand, contract_rows, preferred_element_type=jnp.float32),
        "dp",
        scatter_dimension=0,
        tiled=True,
    )
    own_signs = lax.dynamic_slice_in_dim(sign_table, lax.axis_index("dp") * out_rows, out_rows, 0)
    return own_signs.astype(jnp.float32) * (hessian / live_count)


def solution(mesh):
    in_specs = (
        P(("dp", "tensor"), None),
        P(("dp", "tensor"), None),
        P(("dp", "tensor")),
        P(None, "tensor"),
        P(None, "tensor"),
        P("tensor", None),
        P(),
    )
    out_specs = P("dp", "tensor")
    return jax.shard_map(
        per_device, mesh=mesh, in_specs=in_specs, out_specs=out_specs, check_vma=False
    )
```

profile of v0, /device:TPU:1, one launch (start us, length us, event | category | flops | bytes accessed | tf_op | source)
XLA Modules:
  0.0 291.0 jit_solution(9189681007187733209)
XLA Ops:
  6.5 0.0 all-gather.5.cloned.1.call-start
  6.5 0.7 all-gather.5.cloned.1.call-update
  7.3 0.0 all-gather.3.cloned.1.call-start
  7.3 0.7 convert_element_type.16
  8.0 1.6 broadcast_multiply_fusion
  9.6 0.0 all-gather.3.cloned.1.call-update
  9.6 0.0 reduce-scatter.2.cloned.1.call-start
  10.4 82.6 %all-gather.5.cloned.1.call-done = bf16[512,4096]{1,0:T(8,128)(2,1)} async-done(((bf16[16,4096]{1,0:T(8,128)(2,1)}), bf16[512,4096]{1,0:T(8,128)(2,1)}) %all-gather.5.cloned.1.call-update) | async-done | bytes 4194320 | tf_op jit(solution)/shard_map/all_gather | solution.py:43
  92.9 5.4 %fusion.29 = f32[512,448]{0,1:T(8,128)S(1)} fusion(bf16[512,4096]{1,0:T(8,128)(2,1)} %all-gather.5.cloned.1.call-done, bf16[4096,448]{0,1:T(8,128)(2,1)} %param.10), kind=kOutput, calls=%fused_computation.37 | convolution fusion | flops 1879048192 | bytes 8781824 | tf_op jit(solution)/shard_map/dot_general | solution.py:46
  98.3 76.3 %all-gather.3.cloned.1.call-done = bf16[512,4096]{1,0:T(8,128)(2,1)} async-done(((bf16[16,4096]{1,0:T(8,128)(2,1)}), bf16[512,4096]{1,0:T(8,128)(2,1)}) %all-gather.3.cloned.1.call-update) | async-done | bytes 4194320 | tf_op jit(solution)/shard_map/all_gather | solution.py:44
  174.6 0.0 copy-start
  174.6 5.5 %fusion.28 = f32[512,448]{0,1:T(8,128)S(1)} fusion(bf16[512,4096]{1,0:T(8,128)(2,1)} %all-gather.3.cloned.1.call-done, bf16[448,4096]{1,0:T(8,128)(2,1)} %param.12), kind=kOutput, calls=%fused_computation.36 | convolution fusion | flops 1879048192 | bytes 8781824 | tf_op jit(solution)/shard_map/dot_general | solution.py:49
  180.2 0.0 copy-done
  180.2 4.3 %fusion.10 = f32[512,448]{0,1:T(8,128)S(1)} fusion(bf16[512,4096]{1,0:T(8,128)(2,1)S(1)} %copy-done, s32[]{:T(128)} %bitcast, s32[448]{0:T(512)S(1)} %iota_add_fusion, s32[4096]{0:T(1024)S(1)} %iota_multiply_fusion), kind=kOutput, calls=%fused_computation.15 | convolution fusion | flops 1908408320 | bytes 5129988 | tf_op jit(solution)/shard_map/dot_general | solution.py:48
  184.4 11.8 %convolution_bitcast_fusion = f32[4096,448]{0,1:T(8,128)} fusion(bf16[512,4096]{1,0:T(8,128)(2,1)} %all-gather.5.cloned.1.call-done, f32[512,448]{0,1:T(8,128)S(1)} %fusion.10, f32[512,448]{0,1:T(8,128)S(1)} %fusion.28, bf16[4096,448]{0,1:T(8,128)(2,1)} %param.11, f32[512,448]{0,1:T(8,128)S(1)} %fusion.29), kind=kOutput, calls=%fused_computation.9 | convolution fusion | flops 3761307648 | bytes 17956864 | tf_op jit(solution)/shard_map/dot_general | solution.py:54
  196.2 0.0 copy-start.1
  196.2 0.0 reduce-scatter.2.cloned.1.call-update
  196.2 0.6 copy-done.1
  196.9 0.6 convert_reduce_fusion
  197.5 78.3 %psum.7 = f32[]{:T(128)} all-reduce(f32[]{:T(128)} %convert_reduce_fusion), channel_id=1, replica_groups=mesh['dp'=8,'tensor'=32] {'dp','tensor'}, use_global_device_ids=true, to_apply=%region_2.0 | all-reduce | flops 1 | bytes 8 | tf_op jit(solution)/shard_map/psum | solution.py:45
  275.7 5.6 %fusion.5 = s32[4096,448]{0,1:T(8,128)} fusion(s32[]{:T(128)} %bitcast, s32[448]{0:T(512)S(1)} %iota_add_fusion, s32[4096]{0:T(1024)S(1)} %iota_multiply_fusion), kind=kLoop, calls=%fused_computation.8 | loop fusion | flops 27525120 | bytes 7358212 | tf_op jit(solution)/shard_map/sub | solution.py:25
  281.3 0.0 reduce-scatter.2.cloned.1.call-done
  281.3 3.1 %divide_multiply_fusion = f32[512,448]{0,1:T(8,128)} fusion(f32[512,448]{0,1:T(8,128)} %reduce-scatter.2.cloned.1.call-done, s32[4096,448]{0,1:T(8,128)} %fusion.5, s32[]{:T(128)S(6)} %select_n.3, f32[]{:T(128)} %psum.7), kind=kLoop, calls=%fused_computation.19 | loop fusion | flops 688128 | bytes 2752520 | tf_op jit(solution)/shard_map/mul | solution.py:60
  (2 shorter events, 0.0 us)
Async XLA Ops:
  6.5 86.4 %all-gather.5.cloned.1.call-start = ((), (), s32[]{:S(2)}) async-start(), calls=%async_computation.2 | async-start | bytes 4325376 | tf_op jit(solution)/shard_map/all_gather | solution.py:43
  7.3 167.3 %all-gather.3.cloned.1.call-start = ((), (), s32[]{:S(2)}) async-start(), calls=%async_computation.1 | async-start | bytes 4325376 | tf_op jit(solution)/shard_map/all_gather | solution.py:44
  9.6 271.7 %reduce-scatter.2.cloned.1.call-start = ((), (), s32[]{:S(2)}) async-start(), calls=%async_computation.3 | async-start | bytes 8257536 | tf_op jit(solution)/shard_map/reduce_scatter | solution.py:53
  174.6 5.5 %copy-start = (bf16[512,4096]{1,0:T(8,128)(2,1)S(1)}, bf16[512,4096]{1,0:T(8,128)(2,1)}, u32[]{:S(2)}) copy-start(bf16[512,4096]{1,0:T(8,128)(2,1)} %all-gather.5.cloned.1.call-done) | copy-start | bytes 12582916
  196.2 0.7 copy-start.1
Sparse Core Ops, SparseCore 0:
  9.9 82.9 all-gather.4
  95.5 79.0 all-gather.2
  196.4 49.7 reduce-scatter.1
where the time goes:
time: 291 us
  waiting for transfers between devices  160 us (55%)
  blocking collectives  78.3 us (27%)
  matrix products  27 us (9%)
  between operations  13.8 us (5%)
  other arithmetic  11.7 us (4%)
    all_gather x1, waiting for transfers between devices, per_device(): features = lax.all_gather(tokens, 'tensor', axis=0, tiled=True)  82.6 us
    psum x1, blocking collectives, per_device(): lax.psum(jnp.sum(live_flags.astype(jnp.float32)), ('dp', 'tensor'))  78.3 us
    all_gather x1, waiting for transfers between devices, per_device(): masked_rows = lax.all_gather(masked, 'tensor', axis=0, tiled=True)  76.3 us
    dot_general x1, matrix products, per_device(): lax.dot_general(features, operand, contract_rows, preferred_element_type=...  11.8 us
  transfers between devices with their start and end apart: 3, of which 2 were waited for; matrix products, arithmetic and copies ran while one was open for 5% of the time, Pallas kernels for 0%

commit v1 on v0

v1 whole, which is shorter than its diff:
```python
import jax
import jax.numpy as jnp
from jax import lax
from jax.experimental import pallas as pl
from jax.experimental.pallas import tpu as pltpu
from jax.sharding import PartitionSpec as P

FF = 14336
D = 4096
NY, NZ, NX = 4, 8, 4
ROWS = 16
WIDTH = 448
CHUNK = 128
N_CHUNK = 4
OUT_ROWS = 512
HALF = WIDTH // 2
MASK_AT = 2 * D
WIDE = 2 * D + 128
FAM = ((0, 3328), (3328, WIDE - 3328))
DZ = (0, 1, -1, 2, -2, 3, -3, 4)
DY = (0, 1, -1, 2)
MESH = pl.DeviceIdType.MESH
NT = (((1,), (1,)), ((), ()))
TN = (((0,), (0,)), ((), ()))
F32 = jnp.float32
BF16 = jnp.bfloat16


def slot(dy, dz):
    return DZ.index(dz) * 4 + DY.index(dy)


def arrival_order():
    order = [(-1, 0, 0), (1, 0, 0), (0, -1, 0), (0, 1, 0), (0, -1, 1), (0, 1, 1), (-1, 0, 1), (1, 0, 1), (2, 0, 0)]
    for s in (1, 2, 3):
        order += [(-1, -s, 0), (-1, s, 0), (1, -s, 0), (1, s, 0), (-1, -s, 1), (1, -s, 1)]
        order += [(0, -s - 1, 0), (0, s + 1, 0)] if s < 3 else [(0, 4, 0)]
        order += [(-1, s, 1), (1, s, 1)]
        if s == 1:
            order += [(2, 0, 1)]
        order += [(0, -s - 1, 1), (0, s + 1, 1)] if s < 3 else [(0, 4, 1)]
        order += [(2, -s, 1), (2, -s, 0), (2, s, 0), (2, s, 1)]
    order += [(-1, 4, 0), (1, 4, 0), (-1, 4, 1), (1, 4, 1), (2, 4, 0), (2, 4, 1)]
    return order


def curvature(gate_pre):
    sigmoid_val = jax.nn.sigmoid(gate_pre)
    return sigmoid_val * (1.0 - sigmoid_val) * (2.0 + gate_pre * (1.0 - 2.0 * sigmoid_val))


def kernel(
    tok_ref, cot_ref, mask_ref, seed_ref, wg_hbm, wu_hbm, wd_hbm, out_ref,
    x, cot, wg, wu, wd, sign, gate, up, tan, op, own, core_out, core_in, x_out, x_in, cnt_out, cnt_in,
    local_sem, ag_send, ag_recv, core_send, core_recv, x_send, x_recv, cnt_send, cnt_recv,
):
    dp = lax.axis_index("dp")
    me = lax.axis_index("tensor")
    core = lax.rem(dp, 2)
    xi = lax.div(dp, 2)
    yi = lax.div(me, NZ)
    zi = lax.rem(me, NZ)

    def at_y(step):
        return dp, lax.rem(yi + step + NY, NY) * NZ + zi

    def at_z(step):
        return dp, yi * NZ + lax.rem(zi + step + NZ, NZ)

    def at_x(step):
        return lax.rem(xi + step + NX, NX) * 2 + core, me

    partner = (xi * 2 + 1 - core, me)
    away = 1 - 2 * core

    tok_copy = pltpu.make_async_copy(tok_ref, x.at[pl.ds(0, ROWS), pl.ds(0, D)], local_sem.at[0])
    cot_copy = pltpu.make_async_copy(cot_ref, cot, local_sem.at[1])
    wg_copy = pltpu.make_async_copy(wg_hbm, wg, local_sem.at[2])
    wu_copy = pltpu.make_async_copy(wu_hbm, wu, local_sem.at[3])
    wd_copy = pltpu.make_async_copy(wd_hbm, wd, local_sem.at[4])
    tok_copy.start()
    cot_copy.start()

    peers = [at_y(1), at_y(-1), at_z(1), at_z(-1), partner, at_x(1), at_x(-1), at_x(2)]
    barrier = pltpu.get_barrier_semaphore()
    for peer in peers:
        pl.semaphore_signal(barrier, inc=1, device_id=peer, device_id_type=MESH)

    row = lax.broadcasted_iota(jnp.int32, (ROWS, 128), 0)
    live = jnp.zeros((ROWS, 128), F32)
    for r in range(ROWS):
        live = jnp.where(row == r, mask_ref[r].astype(F32), live)
    x[0:ROWS, MASK_AT:WIDE] = live.astype(BF16)
    cot_copy.wait()
    x[0:ROWS, D:MASK_AT] = (cot[...].astype(F32) * live[:, 0:1]).astype(BF16)
    tok_copy.wait()
    pl.semaphore_wait(barrier, len(peers))

    def block(at, fam):
        start, size = FAM[fam]
        if not isinstance(at, int):
            return x.at[pl.ds(pl.multiple_of(at * ROWS, ROWS), ROWS), pl.ds(start, size)]
        return x.at[pl.ds(at * ROWS, ROWS), pl.ds(start, size)]

    def hop(fam, src, dst, device):
        return pltpu.make_async_remote_copy(
            src_ref=block(src, fam),
            dst_ref=block(dst, fam),
            send_sem=ag_send.at[fam, dst],
            recv_sem=ag_recv.at[fam, dst],
            device_id=device,
            device_id_type=MESH,
        )

    def z_sends(dy, dz, fam):
        if dz <= 0 and dz > -3:
            hop(fam, slot(dy, dz), slot(dy, dz - 1), at_z(1)).start()
        if dz >= 0 and dz < 3:
            hop(fam, slot(dy, dz), slot(dy, dz + 1), at_z(-1)).start()
        if dz == 3:
            hop(fam, DZ.index(-3) * 4 + DY.index(dy) - 4 * core, slot(dy, 4), at_z(away)).start()

    def y_sends(dy, dz, fam):
        if dy == 0:
            hop(fam, slot(0, dz), slot(-1, dz), at_y(1)).start()
            hop(fam, slot(0, dz), slot(1, dz), at_y(-1)).start()
        if dy == 1:
            hop(fam, DZ.index(dz) * 4 + 2 - core, slot(2, dz), at_y(away)).start()

    y_sends(0, 0, 0)
    z_sends(0, 0, 0)
    z_sends(0, 0, 1)
    y_sends(0, 0, 1)
    wg_copy.start()
    wu_copy.start()
    wd_copy.start()

    first_col = me * WIDTH
    col_term = (lax.broadcasted_iota(jnp.int32, (1, WIDTH), 1) + first_col) * jnp.int32(-1640531535)
    col_term = col_term + seed_ref[0] * jnp.int32(668265263)

    def make_signs(k):
        def run():
            size = D // 16
            i = lax.broadcasted_iota(jnp.int32, (size, 1), 0) + k * size
            h = (i * FF) * jnp.int32(-1640531535) + col_term
            h = h ^ lax.shift_right_logical(h, jnp.full_like(h, 15))
            h = h * jnp.int32(739982445)
            h = h ^ lax.shift_right_logical(h, jnp.full_like(h, 12))
            h = h * jnp.int32(695872825)
            h = h ^ lax.shift_left(h, jnp.full_like(h, 15))
            sign[k * size : (k + 1) * size, :] = jnp.where(h < 0, F32(-1.0), F32(1.0)).astype(BF16)

        return run

    def tokens_of(c):
        return slice(c * CHUNK, (c + 1) * CHUNK)

    def make_gate(c):
        def run():
            if c == 0:
                wg_copy.wait()
            gate[...] = jnp.dot(x[tokens_of(c), 0:D], wg[...], preferred_element_type=F32)

        return run

    def make_up(c):
        def run():
            if c == 0:
                wu_copy.wait()
            up[...] = jnp.dot(x[tokens_of(c), 0:D], wu[...], preferred_element_type=F32)

        return run

    def make_tan(c):
        def run():
            tan[...] = jnp.dot(x[tokens_of(c), 0:D], sign[...], preferred_element_type=F32)

        return run

    def make_op(c):
        def run():
            if c == 0:
                wd_copy.wait()
            back = lax.dot_general(x[tokens_of(c), D:MASK_AT], wd[...], NT, preferred_element_type=F32)
            operand = back * up[...] * curvature(gate[...]) * tan[...]
            op[tokens_of(c), :] = operand.astype(BF16)

        return run

    order = arrival_order()
    here = {(0, 0, 0), (0, 0, 1)}
    work = [(None, make_signs(k)) for k in range(16)]
    for c in range(N_CHUNK):
        needs = {(dy, dz, fam) for dz in DZ[2 * c : 2 * c + 2] for dy in DY for fam in (0, 1)}
        work += [(needs, make_gate(c)), (needs, make_up(c)), (needs, make_tan(c)), (needs, make_op(c))]
    for dy, dz, fam in order:
        hop(fam, 0, slot(dy, dz), partner).wait_recv()
        here.add((dy, dz, fam))
        if fam == 0:
            if dy == 1 and dz == 0:
                y_sends(1, 0, 0)
            z_sends(dy, dz, 0)
        else:
            if dy == 0:
                z_sends(0, dz, 1)
                y_sends(0, dz, 1)
            elif dy == 1:
                y_sends(1, dz, 1)
        if work and (work[0][0] is None or work[0][0] <= here):
            work.pop(0)[1]()
    for _, run in work:
        run()

    count = jnp.sum(x[:, MASK_AT:WIDE].astype(F32), axis=0, keepdims=True)
    cnt_out[0] = jnp.broadcast_to(count, (8, 128))

    def count_copy(src, dst, device):
        return pltpu.make_async_remote_copy(
            src_ref=cnt_out.at[src],
            dst_ref=cnt_in.at[dst],
            send_sem=cnt_send.at[dst],
            recv_sem=cnt_recv.at[dst],
            device_id=device,
            device_id_type=MESH,
        )

    count_copy(0, 0, partner).start()

    def core_copy(k):
        return pltpu.make_async_remote_copy(
            src_ref=core_out.at[k],
            dst_ref=core_in.at[k],
            send_sem=core_send.at[k],
            recv_sem=core_recv.at[k],
            device_id=partner,
            device_id_type=MESH,
        )

    def rows_of(half):
        return pl.ds(half * HALF, HALF)

    def x_copy(k, half, dst, device):
        return pltpu.make_async_remote_copy(
            src_ref=x_out.at[k - 1, rows_of(half)],
            dst_ref=x_in.at[dst, rows_of(half)],
            send_sem=x_send.at[k - 1, half],
            recv_sem=x_recv.at[dst, half],
            device_id=device,
            device_id_type=MESH,
        )

    def product(k, of_core):
        start = (lax.rem(xi + k, NX) * 2 + of_core) * OUT_ROWS
        cols = pl.ds(pl.multiple_of(start, OUT_ROWS), OUT_ROWS)
        return lax.dot_general(op[...], x[:, cols], TN, preferred_element_type=F32)

    for k in (2, 1, 3, 0):
        core_out[k] = product(k, 1 - core).astype(BF16)
        core_copy(k).start()
        own[k] = product(k, core)
        if k == 2:
            continue
        last = {1: 2, 3: 1, 0: 3}[k]
        core_copy(last).wait_recv()
        own[last] += core_in[last].astype(F32)
        if last == 2:
            x_out[1] = own[2].astype(BF16)
            x_copy(2, 0, 1, at_x(1)).start()
            x_copy(2, 1, 1, at_x(-1)).start()
        elif last == 1:
            x_out[0, HALF:WIDTH] = own[1, HALF:WIDTH].astype(BF16)
            x_copy(1, 1, 0, at_x(1)).start()
        elif last == 3:
            x_out[2, 0:HALF] = own[3, 0:HALF].astype(BF16)
            x_copy(3, 0, 2, at_x(-1)).start()
    count_copy(0, 0, partner).wait_recv()
    pair = cnt_out[0] + cnt_in[0]
    cnt_out[1] = pair
    count_copy(1, 1, at_x(1)).start()
    count_copy(1, 2, at_x(2)).start()
    count_copy(1, 3, at_x(-1)).start()
    core_copy(0).wait_recv()
    own[0] += core_in[0].astype(F32)

    x_copy(2, 0, 1, at_x(1)).wait_recv()
    x_out[0, 0:HALF] = (own[1, 0:HALF] + x_in[1, 0:HALF].astype(F32)).astype(BF16)
    x_copy(1, 0, 0, at_x(1)).start()
    x_copy(2, 1, 1, at_x(-1)).wait_recv()
    x_out[2, HALF:WIDTH] = (own[3, HALF:WIDTH] + x_in[1, HALF:WIDTH].astype(F32)).astype(BF16)
    x_copy(3, 1, 2, at_x(-1)).start()

    for d in (1, 2, 3):
        count_copy(1, d, at_x(1)).wait_recv()
    total = pair + cnt_in[1] + cnt_in[2] + cnt_in[3]
    live_count = total[0:1, 0:1]
    x_copy(1, 1, 0, at_x(1)).wait_recv()
    x_copy(3, 0, 2, at_x(-1)).wait_recv()
    x_copy(1, 0, 0, at_x(1)).wait_recv()
    x_copy(3, 1, 2, at_x(-1)).wait_recv()
    hess = own[0] + x_in[0].astype(F32) + x_in[2].astype(F32)
    own_signs = sign[pl.ds(pl.multiple_of(dp * OUT_ROWS, OUT_ROWS), OUT_ROWS), :].astype(F32)
    out_ref[...] = own_signs * (hess.T / live_count)

    for dy, dz, fam in order:
        hop(fam, 0, slot(dy, dz), partner).wait_send()
    for k in range(4):
        core_copy(k).wait_send()
    for k in (1, 2, 3):
        for half in (0, 1):
            x_copy(k, half, 0, at_x(1)).wait_send()
    for d in range(4):
        count_copy(0, d, at_x(1)).wait_send()


def per_device(tokens, cotangent, loss_mask, gate_weight, up_weight, down_weight, probe_seed):
    any_space = pl.BlockSpec(memory_space=pl.ANY)
    smem = pl.BlockSpec(memory_space=pltpu.SMEM)
    vmem = pltpu.VMEM
    dma = pltpu.SemaphoreType.DMA
    return pl.pallas_call(
        kernel,
        out_shape=jax.ShapeDtypeStruct((OUT_ROWS, WIDTH), F32),
        in_specs=[any_space, any_space, smem, smem, any_space, any_space, any_space],
        out_specs=pl.BlockSpec(memory_space=vmem),
        scratch_shapes=[
            vmem((NY * NZ * ROWS, WIDE), BF16),
            vmem((ROWS, D), BF16),
            vmem((D, WIDTH), BF16),
            vmem((D, WIDTH), BF16),
            vmem((WIDTH, D), BF16),
            vmem((D, WIDTH), BF16),
            vmem((CHUNK, WIDTH), F32),
            vmem((CHUNK, WIDTH), F32),
            vmem((CHUNK, WIDTH), F32),
            vmem((N_CHUNK * CHUNK, WIDTH), BF16),
            vmem((4, WIDTH, OUT_ROWS), F32),
            vmem((4, WIDTH, OUT_ROWS), BF16),
            vmem((4, WIDTH, OUT_ROWS), BF16),
            vmem((3, WIDTH, OUT_ROWS), BF16),
            vmem((3, WIDTH, OUT_ROWS), BF16),
            vmem((2, 8, 128), F32),
            vmem((4, 8, 128), F32),
            dma((5,)),
            dma((2, NY * NZ)),
            dma((2, NY * NZ)),
            dma((4,)),
            dma((4,)),
            dma((3, 2)),
            dma((3, 2)),
            dma((4,)),
            dma((4,)),
        ],
        compiler_params=pltpu.CompilerParams(
            collective_id=0, has_side_effects=True, vmem_limit_bytes=56 * 2**20
        ),
        cost_estimate=pl.CostEstimate(flops=9_400_000_000, bytes_accessed=12_000_000, transcendentals=230_000),
    )(tokens, cotangent, loss_mask, probe_seed, gate_weight, up_weight, down_weight)


def solution(mesh):
    in_specs = (
        P(("dp", "tensor"), None),
        P(("dp", "tensor"), None),
        P(("dp", "tensor")),
        P(None, "tensor"),
        P(None, "tensor"),
        P("tensor", None),
        P(),
    )
    return jax.shard_map(
        per_device, mesh=mesh, in_specs=in_specs, out_specs=P("dp", "tensor"), check_vma=False
    )
```

time: 291 us -> 107 us (0.37)
  waiting for transfers between devices: 160 us -> 0 us
  Pallas kernels: 0 us -> 90.1 us
  blocking collectives: 78.3 us -> 0 us
  matrix products: 27 us -> 0 us
  local copies, waits for them, and re-layouts: 0.63 us -> 15.4 us
  between operations: 13.8 us -> 0.66 us
  other arithmetic: 11.7 us -> 0 us
    all_gather x2 -> x0, waiting for transfers between devices: 159 us -> none  [the longest x1 82.6 us: per_device(): features = lax.all_gather(tokens, 'tensor', axis=0, tiled=True)]
    pallas_call x0 -> x1, Pallas kernels: none -> 90.1 us  [per_device(): pl.pallas_call(kernel, out_shape=jax.ShapeDtypeStruct((OUT_ROWS, WIDTH),...]
    psum x1 -> x0, blocking collectives: 78.3 us -> none  [per_device(): lax.psum(jnp.sum(live_flags.astype(jnp.float32)), ('dp', 'tensor'))]
    dot_general x4 -> x0, matrix products: 27 us -> none  [the longest x1 11.8 us: per_device(): lax.dot_general(features, operand, contract_rows, preferred_element_type=...]
    unnamed x4 -> x2, local copies, waits for them, and re-layouts: 0.63 us -> 12.9 us
    sub x1 -> x0, other arithmetic: 5.61 us -> none  [probe_signs(): return jnp.int32(1) - jnp.int32(2) * lowbit]
    mul x3 -> x0, other arithmetic: 4.79 us -> none  [the longest x1 3.14 us: per_device(): return own_signs.astype(jnp.float32) * (hessian / live_count)]
  transfers between devices with their start and end apart: 3 -> 0, of which waited for: 2 -> 0; matrix products, arithmetic and copies ran while one was open for 5% -> 0% of each run, Pallas kernels for 0% -> 0%
where the time goes in v1:
time: 107 us; the launch traced here: 106 us
  Pallas kernels  90.1 us (84%)
  local copies, waits for them, and re-layouts  15.4 us (14%)
    pallas_call x1, Pallas kernels, per_device(): pl.pallas_call(kernel, out_shape=jax.ShapeDtypeStruct((OUT_ROWS, WIDTH),...  90.1 us
    unnamed x2, local copies, waits for them, and re-layouts  12.9 us
    pallas_call x1, local copies, waits for them, and re-layouts, per_device(): pl.pallas_call(kernel, out_shape=jax.ShapeDtypeStruct((OUT_ROWS, WIDTH),...  2.47 us

profile of v1, /device:TPU:1, one launch (start us, length us, event | category | flops | bytes accessed | tf_op | source)
XLA Modules:
  0.0 106.1 jit_solution(9366325375842730765)
XLA Ops:
  0.7 6.4 %copy.8.wg_hbm = bf16[4096,448]{1,0:T(8,128)(2,1)} copy(bf16[4096,448]{0,1:T(8,128)(2,1)} %param.10) | data formatting | bytes 7340032 | tf_op args[3]
  7.1 6.5 %copy.9.wu_hbm = bf16[4096,448]{1,0:T(8,128)(2,1)} copy(bf16[4096,448]{0,1:T(8,128)(2,1)} %param.11) | data formatting | bytes 7340032 | tf_op args[4]
  13.6 90.1 %shard_map.73 = f32[512,448]{1,0:T(8,128)} custom-call(bf16[16,4096]{1,0:T(8,128)(2,1)} %tok_ref.1, bf16[16,4096]{1,0:T(8,128)(2,1)} %cot_ref.1, s32[16]{0:T(128)} %mask_ref.1, s32[1]{0:T(128)S(6)} %copy.11.seed_ref, bf16[4096,448]{1,0:T(8,128)(2,1)} %copy.8.wg_hbm, bf16[4096,448]{1,0:T(8,128)(2,1)} %copy.9.wu_hbm, bf16[448,4096]{1,0:T(8,128)(2,1)} %wd_hbm.1), custom_call_target="tpu_custom_call" | custom-call | flops 9400000512 | bytes 12000000 | tf_op jit(solution)/shard_map/pallas_call | solution.py:321
  103.7 2.5 %copy.10 = f32[512,448]{0,1:T(8,128)} copy(f32[512,448]{1,0:T(8,128)} %shard_map.73) | data formatting | bytes 1835008 | tf_op jit(solution)/shard_map/pallas_call | solution.py:321

commit v2 on v1

--- a/solution.py
+++ b/solution.py
@@ -16,7 +16,8 @@
 HALF = WIDTH // 2
 MASK_AT = 2 * D
 WIDE = 2 * D + 128
-FAM = ((0, 3328), (3328, WIDE - 3328))
+SPLIT = 24 * 128
+FAM = ((0, SPLIT), (SPLIT, WIDE - SPLIT))
 DZ = (0, 1, -1, 2, -2, 3, -3, 4)
 DY = (0, 1, -1, 2)
 MESH = pl.DeviceIdType.MESH
@@ -30,18 +31,30 @@
     return DZ.index(dz) * 4 + DY.index(dy)
 
 
-def arrival_order():
-    order = [(-1, 0, 0), (1, 0, 0), (0, -1, 0), (0, 1, 0), (0, -1, 1), (0, 1, 1), (-1, 0, 1), (1, 0, 1), (2, 0, 0)]
-    for s in (1, 2, 3):
-        order += [(-1, -s, 0), (-1, s, 0), (1, -s, 0), (1, s, 0), (-1, -s, 1), (1, -s, 1)]
-        order += [(0, -s - 1, 0), (0, s + 1, 0)] if s < 3 else [(0, 4, 0)]
-        order += [(-1, s, 1), (1, s, 1)]
-        if s == 1:
-            order += [(2, 0, 1)]
-        order += [(0, -s - 1, 1), (0, s + 1, 1)] if s < 3 else [(0, 4, 1)]
-        order += [(2, -s, 1), (2, -s, 0), (2, s, 0), (2, s, 1)]
-    order += [(-1, 4, 0), (1, 4, 0), (-1, 4, 1), (1, 4, 1), (2, 4, 0), (2, 4, 1)]
-    return order
+PLAN = (
+    (2, 0, 0, 0), (2, 1, 0, 0), (1, -1, 0, 0), (1, 0, -1, 0), (1, 1, 0, 0), (2, 2, 0, 0), (1, 0, -1, 1),
+    (1, -1, 0, 1), (2, 3, 0, 0), (2, 4, 0, 0), (1, 0, 1, 1), (2, 5, 0, 0), (2, 6, 0, 0), (2, 7, 0, 0),
+    (1, 1, 0, 1), (1, 0, 1, 0), (0, -1, 0, 0), (1, 2, 0, 0), (0, 0, -1, 1), (1, 0, -2, 1), (0, -1, 0, 1),
+    (1, 2, 0, 1), (1, -1, -1, 1), (0, 0, 1, 1), (1, 0, 2, 1), (1, -1, -1, 0), (1, 1, -1, 1), (0, 0, -2, 1),
+    (1, 0, -3, 1), (1, -1, 1, 1), (0, 0, 2, 1), (1, 0, 3, 1), (1, 1, 1, 1), (1, -1, 1, 0), (0, -1, -1, 1),
+    (1, 2, -1, 1), (0, 0, -3, 1), (1, 0, 4, 1), (0, -1, 1, 1), (1, 2, 1, 1), (0, 1, 0, 0), (1, 1, -1, 0),
+    (1, 1, 1, 0), (1, -1, -2, 1), (0, 2, 0, 0), (1, 2, -1, 0), (1, 1, -2, 1), (1, 2, 1, 0), (0, 0, -1, 0),
+    (1, 0, -2, 0), (1, -1, 2, 1), (0, 0, 1, 0), (1, 0, 2, 0), (0, -1, -1, 0), (1, -1, -2, 0), (1, 1, 2, 1),
+    (0, -1, 1, 0), (1, -1, 2, 0), (0, -1, -2, 1), (1, 2, -2, 1), (0, 1, -1, 0), (1, 1, -2, 0), (0, 1, 0, 1),
+    (0, 2, 0, 1), (0, 1, 1, 1), (0, 2, 1, 1), (0, 1, 1, 0), (0, 2, 1, 0), (2, 8, 0, 0), (1, 1, 2, 0),
+    (2, 9, 0, 0), (0, -1, 2, 1), (1, 2, 2, 1), (0, 2, -1, 0), (1, 2, -2, 0), (2, 10, 0, 0), (1, -1, -3, 1),
+    (1, 2, 2, 0), (2, 11, 0, 0), (0, 0, -2, 0), (1, 0, -3, 0), (1, 1, -3, 1), (0, 0, 2, 0), (1, 0, 3, 0),
+    (0, -1, -2, 0), (1, -1, -3, 0), (0, 0, 3, 1), (1, -1, 3, 1), (0, -1, 2, 0), (1, -1, 3, 0), (1, 1, 3, 1),
+    (0, 1, -2, 0), (1, 1, -3, 0), (0, 1, -1, 1), (0, 2, -1, 1), (0, 1, 2, 1), (0, 1, 2, 0), (0, 2, 2, 1),
+    (0, 2, 2, 0), (2, 12, 0, 0), (1, 1, 3, 0), (0, -1, -3, 1), (1, 2, -3, 1), (2, 13, 0, 0), (0, 2, -2, 0),
+    (1, 2, -3, 0), (2, 14, 0, 0), (1, 2, 3, 0), (0, -1, 3, 1), (1, 2, 3, 1), (2, 15, 0, 0), (0, 0, -3, 0),
+    (1, 0, 4, 0), (0, 0, 4, 1), (1, -1, 4, 1), (0, -1, -3, 0), (1, -1, 4, 0), (0, 1, -3, 0), (1, 1, 4, 0),
+    (1, 1, 4, 1), (0, 2, -3, 0), (1, 2, 4, 0), (0, 1, -2, 1), (0, 2, -2, 1), (0, 0, 3, 0), (0, -1, 3, 0),
+    (0, 1, 3, 1), (0, 1, 3, 0), (0, 2, 3, 0), (0, 2, 3, 1), (2, 16, 0, 0), (2, 17, 0, 0), (0, -1, 4, 1),
+    (1, 2, 4, 1), (2, 18, 0, 0), (2, 19, 0, 0), (0, 0, 4, 0), (0, -1, 4, 0), (0, 1, 4, 0), (0, 2, 4, 0),
+    (2, 20, 0, 0), (2, 21, 0, 0), (2, 22, 0, 0), (0, 1, -3, 1), (0, 2, -3, 1), (0, 1, 4, 1), (0, 2, 4, 1),
+    (2, 23, 0, 0), (2, 24, 0, 0), (2, 25, 0, 0), (2, 26, 0, 0),
+)
 
 
 def curvature(gate_pre):
@@ -61,17 +74,18 @@
     yi = lax.div(me, NZ)
     zi = lax.rem(me, NZ)
 
+    away = 1 - 2 * core
+
     def at_y(step):
-        return dp, lax.rem(yi + step + NY, NY) * NZ + zi
+        return dp, lax.rem(yi + away * step + NY, NY) * NZ + zi
 
     def at_z(step):
-        return dp, yi * NZ + lax.rem(zi + step + NZ, NZ)
+        return dp, yi * NZ + lax.rem(zi + away * step + NZ, NZ)
 
     def at_x(step):
         return lax.rem(xi + step + NX, NX) * 2 + core, me
 
     partner = (xi * 2 + 1 - core, me)
-    away = 1 - 2 * core
 
     tok_copy = pltpu.make_async_copy(tok_ref, x.at[pl.ds(0, ROWS), pl.ds(0, D)], local_sem.at[0])
     cot_copy = pltpu.make_async_copy(cot_ref, cot, local_sem.at[1])
@@ -98,13 +112,16 @@
 
     def block(at, fam):
         start, size = FAM[fam]
-        if not isinstance(at, int):
-            return x.at[pl.ds(pl.multiple_of(at * ROWS, ROWS), ROWS), pl.ds(start, size)]
         return x.at[pl.ds(at * ROWS, ROWS), pl.ds(start, size)]
 
-    def hop(fam, src, dst, device):
+    def hop(dy, dz, fam):
+        if dy != 0 and (fam == 1 or dz == 0):
+            came_dy, came_dz, device = (0, dz, at_y(-dy)) if dy != 2 else (-1, dz, at_y(1))
+        else:
+            came_dy, came_dz, device = (dy, dz - 1, at_z(-1)) if 0 < dz < 4 else (dy, (dz + 1 if dz < 0 else -3), at_z(1))
+        dst = slot(dy, dz)
         return pltpu.make_async_remote_copy(
-            src_ref=block(src, fam),
+            src_ref=block(slot(came_dy, came_dz), fam),
             dst_ref=block(dst, fam),
             send_sem=ag_send.at[fam, dst],
             recv_sem=ag_recv.at[fam, dst],
@@ -112,69 +129,39 @@
             device_id_type=MESH,
         )
 
-    def z_sends(dy, dz, fam):
-        if dz <= 0 and dz > -3:
-            hop(fam, slot(dy, dz), slot(dy, dz - 1), at_z(1)).start()
-        if dz >= 0 and dz < 3:
-            hop(fam, slot(dy, dz), slot(dy, dz + 1), at_z(-1)).start()
-        if dz == 3:
-            hop(fam, DZ.index(-3) * 4 + DY.index(dy) - 4 * core, slot(dy, 4), at_z(away)).start()
-
-    def y_sends(dy, dz, fam):
-        if dy == 0:
-            hop(fam, slot(0, dz), slot(-1, dz), at_y(1)).start()
-            hop(fam, slot(0, dz), slot(1, dz), at_y(-1)).start()
-        if dy == 1:
-            hop(fam, DZ.index(dz) * 4 + 2 - core, slot(2, dz), at_y(away)).start()
-
-    y_sends(0, 0, 0)
-    z_sends(0, 0, 0)
-    z_sends(0, 0, 1)
-    y_sends(0, 0, 1)
     wg_copy.start()
     wu_copy.start()
     wd_copy.start()
-
     first_col = me * WIDTH
-    col_term = (lax.broadcasted_iota(jnp.int32, (1, WIDTH), 1) + first_col) * jnp.int32(-1640531535)
+    col_term = (lax.broadcasted_iota(jnp.int32, (WIDTH, 1), 0) + first_col) * jnp.int32(-1640531535)
     col_term = col_term + seed_ref[0] * jnp.int32(668265263)
 
     def make_signs(k):
         def run():
-            size = D // 16
-            i = lax.broadcasted_iota(jnp.int32, (size, 1), 0) + k * size
+            size = D // 8
+            i = lax.broadcasted_iota(jnp.int32, (1, size), 1) + k * size
             h = (i * FF) * jnp.int32(-1640531535) + col_term
             h = h ^ lax.shift_right_logical(h, jnp.full_like(h, 15))
             h = h * jnp.int32(739982445)
             h = h ^ lax.shift_right_logical(h, jnp.full_like(h, 12))
             h = h * jnp.int32(695872825)
             h = h ^ lax.shift_left(h, jnp.full_like(h, 15))
-            sign[k * size : (k + 1) * size, :] = jnp.where(h < 0, F32(-1.0), F32(1.0)).astype(BF16)
+            sign[:, k * size : (k + 1) * size] = jnp.where(h < 0, F32(-1.0), F32(1.0)).astype(BF16)
 
         return run
 
     def tokens_of(c):
         return slice(c * CHUNK, (c + 1) * CHUNK)
 
-    def make_gate(c):
+    def make_dot(c, out, w, copy, cols):
         def run():
-            if c == 0:
-                wg_copy.wait()
-            gate[...] = jnp.dot(x[tokens_of(c), 0:D], wg[...], preferred_element_type=F32)
-
-        return run
-
-    def make_up(c):
-        def run():
-            if c == 0:
-                wu_copy.wait()
-            up[...] = jnp.dot(x[tokens_of(c), 0:D], wu[...], preferred_element_type=F32)
-
-        return run
-
-    def make_tan(c):
-        def run():
-            tan[...] = jnp.dot(x[tokens_of(c), 0:D], sign[...], preferred_element_type=F32)
+            if copy is not None:
+                copy.wait()
+            part = lax.dot_general(x[tokens_of(c), cols], w[:, cols], NT, preferred_element_type=F32)
+            if cols.start == 0:
+                out[...] = part
+            else:
+                out[...] += part
 
         return run
 
@@ -188,29 +175,20 @@
 
         return run
 
-    order = arrival_order()
-    here = {(0, 0, 0), (0, 0, 1)}
-    work = [(None, make_signs(k)) for k in range(16)]
+    work = [make_signs(k) for k in range(8)]
     for c in range(N_CHUNK):
-        needs = {(dy, dz, fam) for dz in DZ[2 * c : 2 * c + 2] for dy in DY for fam in (0, 1)}
-        work += [(needs, make_gate(c)), (needs, make_up(c)), (needs, make_tan(c)), (needs, make_op(c))]
-    for dy, dz, fam in order:
-        hop(fam, 0, slot(dy, dz), partner).wait_recv()
-        here.add((dy, dz, fam))
-        if fam == 0:
-            if dy == 1 and dz == 0:
-                y_sends(1, 0, 0)
-            z_sends(dy, dz, 0)
+        for cols in (slice(0, D),) if c < N_CHUNK - 1 else (slice(0, SPLIT), slice(SPLIT, D)):
+            work.append(make_dot(c, gate, wg, wg_copy if c == 0 else None, cols))
+            work.append(make_dot(c, up, wu, wu_copy if c == 0 else None, cols))
+            work.append(make_dot(c, tan, sign, None, cols))
+        work.append(make_op(c))
+    for what, dy, dz, fam in PLAN:
+        if what == 0:
+            hop(dy, dz, fam).wait_recv()
+        elif what == 1:
+            hop(dy, dz, fam).start()
         else:
-            if dy == 0:
-                z_sends(0, dz, 1)
-                y_sends(0, dz, 1)
-            elif dy == 1:
-                y_sends(1, dz, 1)
-        if work and (work[0][0] is None or work[0][0] <= here):
-            work.pop(0)[1]()
-    for _, run in work:
-        run()
+            work[dy]()
 
     count = jnp.sum(x[:, MASK_AT:WIDE].astype(F32), axis=0, keepdims=True)
     cnt_out[0] = jnp.broadcast_to(count, (8, 128))
@@ -299,11 +277,12 @@
     x_copy(1, 0, 0, at_x(1)).wait_recv()
     x_copy(3, 1, 2, at_x(-1)).wait_recv()
     hess = own[0] + x_in[0].astype(F32) + x_in[2].astype(F32)
-    own_signs = sign[pl.ds(pl.multiple_of(dp * OUT_ROWS, OUT_ROWS), OUT_ROWS), :].astype(F32)
-    out_ref[...] = own_signs * (hess.T / live_count)
-
-    for dy, dz, fam in order:
-        hop(fam, 0, slot(dy, dz), partner).wait_send()
+    own_signs = sign[:, pl.ds(pl.multiple_of(dp * OUT_ROWS, OUT_ROWS), OUT_ROWS)].astype(F32)
+    out_ref[...] = own_signs * (hess / live_count)
+
+    for what, dy, dz, fam in PLAN:
+        if what == 1:
+            hop(dy, dz, fam).wait_send()
     for k in range(4):
         core_copy(k).wait_send()
     for k in (1, 2, 3):
@@ -318,18 +297,18 @@
     smem = pl.BlockSpec(memory_space=pltpu.SMEM)
     vmem = pltpu.VMEM
     dma = pltpu.SemaphoreType.DMA
-    return pl.pallas_call(
+    out = pl.pallas_call(
         kernel,
-        out_shape=jax.ShapeDtypeStruct((OUT_ROWS, WIDTH), F32),
+        out_shape=jax.ShapeDtypeStruct((WIDTH, OUT_ROWS), F32),
         in_specs=[any_space, any_space, smem, smem, any_space, any_space, any_space],
         out_specs=pl.BlockSpec(memory_space=vmem),
         scratch_shapes=[
             vmem((NY * NZ * ROWS, WIDE), BF16),
             vmem((ROWS, D), BF16),
-            vmem((D, WIDTH), BF16),
-            vmem((D, WIDTH), BF16),
             vmem((WIDTH, D), BF16),
-            vmem((D, WIDTH), BF16),
+            vmem((WIDTH, D), BF16),
+            vmem((WIDTH, D), BF16),
+            vmem((WIDTH, D), BF16),
             vmem((CHUNK, WIDTH), F32),
             vmem((CHUNK, WIDTH), F32),
             vmem((CHUNK, WIDTH), F32),
@@ -355,7 +334,8 @@
             collective_id=0, has_side_effects=True, vmem_limit_bytes=56 * 2**20
         ),
         cost_estimate=pl.CostEstimate(flops=9_400_000_000, bytes_accessed=12_000_000, transcendentals=230_000),
-    )(tokens, cotangent, loss_mask, probe_seed, gate_weight, up_weight, down_weight)
+    )(tokens, cotangent, loss_mask, probe_seed, gate_weight.T, up_weight.T, down_weight)
+    return out.T
 
 
 def solution(mesh):

time: 107 us -> 93 us (0.87)
  local copies, waits for them, and re-layouts: 15.4 us -> 2.16 us
    unnamed x2 -> x1, local copies, waits for them, and re-layouts: 12.9 us -> 2.16 us
    pallas_call x1 -> x0, local copies, waits for them, and re-layouts: 2.47 us -> none  [per_device(): pl.pallas_call(kernel, out_shape=jax.ShapeDtypeStruct((OUT_ROWS, WIDTH),...]
where the time goes in v2:
time: 93 us; the launch traced here: 92.8 us
  Pallas kernels  90 us (97%)
  local copies, waits for them, and re-layouts  2.16 us (2%)
    pallas_call x1, Pallas kernels, per_device(): pl.pallas_call(kernel, out_shape=jax.ShapeDtypeStruct((WIDTH, OUT_ROWS),...  90 us
    unnamed x1, local copies, waits for them, and re-layouts  2.16 us

profile of v2, /device:TPU:1, one launch (start us, length us, event | category | flops | bytes accessed | tf_op | source)
XLA Modules:
  0.0 92.8 jit_solution(18419968930199991897)
XLA Ops:
  0.7 90.0 %shard_map.73 = f32[448,512]{1,0:T(8,128)} custom-call(bf16[16,4096]{1,0:T(8,128)(2,1)} %tok_ref.1, bf16[16,4096]{1,0:T(8,128)(2,1)} %cot_ref.1, s32[16]{0:T(128)} %mask_ref.1, s32[1]{0:T(128)S(6)} %copy.9.seed_ref, bf16[448,4096]{1,0:T(8,128)(2,1)} %bitcast.4, bf16[448,4096]{1,0:T(8,128)(2,1)} %bitcast.5, bf16[448,4096]{1,0:T(8,128)(2,1)} %wd_hbm.1), custom_call_target="tpu_custom_call" | custom-call | flops 9400000512 | bytes 12000000 | tf_op jit(solution)/shard_map/pallas_call | solution.py:300
  90.7 2.2 %copy.10 = f32[512,448]{0,1:T(8,128)} copy(f32[512,448]{0,1:T(8,128)} %bitcast.3) | data formatting | bytes 1835008

commit v3 on v2

--- a/solution.py
+++ b/solution.py
@@ -10,19 +10,18 @@
 NY, NZ, NX = 4, 8, 4
 ROWS = 16
 WIDTH = 448
-CHUNK = 128
-N_CHUNK = 4
+CHUNK = 256
+N_CHUNK = 2
 OUT_ROWS = 512
 HALF = WIDTH // 2
 MASK_AT = 2 * D
 WIDE = 2 * D + 128
-SPLIT = 24 * 128
+SPLIT = 25 * 128
 FAM = ((0, SPLIT), (SPLIT, WIDE - SPLIT))
 DZ = (0, 1, -1, 2, -2, 3, -3, 4)
 DY = (0, 1, -1, 2)
 MESH = pl.DeviceIdType.MESH
 NT = (((1,), (1,)), ((), ()))
-TN = (((0,), (0,)), ((), ()))
 F32 = jnp.float32
 BF16 = jnp.bfloat16
 
@@ -32,28 +31,26 @@
 
 
 PLAN = (
-    (2, 0, 0, 0), (2, 1, 0, 0), (1, -1, 0, 0), (1, 0, -1, 0), (1, 1, 0, 0), (2, 2, 0, 0), (1, 0, -1, 1),
-    (1, -1, 0, 1), (2, 3, 0, 0), (2, 4, 0, 0), (1, 0, 1, 1), (2, 5, 0, 0), (2, 6, 0, 0), (2, 7, 0, 0),
-    (1, 1, 0, 1), (1, 0, 1, 0), (0, -1, 0, 0), (1, 2, 0, 0), (0, 0, -1, 1), (1, 0, -2, 1), (0, -1, 0, 1),
-    (1, 2, 0, 1), (1, -1, -1, 1), (0, 0, 1, 1), (1, 0, 2, 1), (1, -1, -1, 0), (1, 1, -1, 1), (0, 0, -2, 1),
-    (1, 0, -3, 1), (1, -1, 1, 1), (0, 0, 2, 1), (1, 0, 3, 1), (1, 1, 1, 1), (1, -1, 1, 0), (0, -1, -1, 1),
-    (1, 2, -1, 1), (0, 0, -3, 1), (1, 0, 4, 1), (0, -1, 1, 1), (1, 2, 1, 1), (0, 1, 0, 0), (1, 1, -1, 0),
-    (1, 1, 1, 0), (1, -1, -2, 1), (0, 2, 0, 0), (1, 2, -1, 0), (1, 1, -2, 1), (1, 2, 1, 0), (0, 0, -1, 0),
-    (1, 0, -2, 0), (1, -1, 2, 1), (0, 0, 1, 0), (1, 0, 2, 0), (0, -1, -1, 0), (1, -1, -2, 0), (1, 1, 2, 1),
-    (0, -1, 1, 0), (1, -1, 2, 0), (0, -1, -2, 1), (1, 2, -2, 1), (0, 1, -1, 0), (1, 1, -2, 0), (0, 1, 0, 1),
-    (0, 2, 0, 1), (0, 1, 1, 1), (0, 2, 1, 1), (0, 1, 1, 0), (0, 2, 1, 0), (2, 8, 0, 0), (1, 1, 2, 0),
-    (2, 9, 0, 0), (0, -1, 2, 1), (1, 2, 2, 1), (0, 2, -1, 0), (1, 2, -2, 0), (2, 10, 0, 0), (1, -1, -3, 1),
-    (1, 2, 2, 0), (2, 11, 0, 0), (0, 0, -2, 0), (1, 0, -3, 0), (1, 1, -3, 1), (0, 0, 2, 0), (1, 0, 3, 0),
-    (0, -1, -2, 0), (1, -1, -3, 0), (0, 0, 3, 1), (1, -1, 3, 1), (0, -1, 2, 0), (1, -1, 3, 0), (1, 1, 3, 1),
-    (0, 1, -2, 0), (1, 1, -3, 0), (0, 1, -1, 1), (0, 2, -1, 1), (0, 1, 2, 1), (0, 1, 2, 0), (0, 2, 2, 1),
-    (0, 2, 2, 0), (2, 12, 0, 0), (1, 1, 3, 0), (0, -1, -3, 1), (1, 2, -3, 1), (2, 13, 0, 0), (0, 2, -2, 0),
-    (1, 2, -3, 0), (2, 14, 0, 0), (1, 2, 3, 0), (0, -1, 3, 1), (1, 2, 3, 1), (2, 15, 0, 0), (0, 0, -3, 0),
-    (1, 0, 4, 0), (0, 0, 4, 1), (1, -1, 4, 1), (0, -1, -3, 0), (1, -1, 4, 0), (0, 1, -3, 0), (1, 1, 4, 0),
-    (1, 1, 4, 1), (0, 2, -3, 0), (1, 2, 4, 0), (0, 1, -2, 1), (0, 2, -2, 1), (0, 0, 3, 0), (0, -1, 3, 0),
-    (0, 1, 3, 1), (0, 1, 3, 0), (0, 2, 3, 0), (0, 2, 3, 1), (2, 16, 0, 0), (2, 17, 0, 0), (0, -1, 4, 1),
-    (1, 2, 4, 1), (2, 18, 0, 0), (2, 19, 0, 0), (0, 0, 4, 0), (0, -1, 4, 0), (0, 1, 4, 0), (0, 2, 4, 0),
-    (2, 20, 0, 0), (2, 21, 0, 0), (2, 22, 0, 0), (0, 1, -3, 1), (0, 2, -3, 1), (0, 1, 4, 1), (0, 2, 4, 1),
-    (2, 23, 0, 0), (2, 24, 0, 0), (2, 25, 0, 0), (2, 26, 0, 0),
+    (2, 0, 0, 0), (2, 1, 0, 0), (2, 2, 0, 0), (2, 3, 0, 0), (2, 4, 0, 0), (2, 5, 0, 0), (2, 6, 0, 0),
+    (2, 7, 0, 0), (0, -1, 0, 0), (1, 2, 0, 0), (0, 0, -1, 1), (1, 0, -2, 1), (1, -1, -1, 1), (1, 1, -1, 1),
+    (1, -1, -1, 0), (1, -1, 1, 0), (0, 0, 1, 1), (1, 0, 2, 1), (1, -1, 1, 1), (0, 1, 0, 0), (1, 1, -1, 0),
+    (1, 1, 1, 1), (1, 1, 1, 0), (0, 2, 0, 0), (1, 2, -1, 0), (0, -1, 0, 1), (1, 2, 0, 1), (1, 2, 1, 0),
+    (0, 0, -2, 1), (1, 0, -3, 1), (1, -1, -2, 1), (0, 0, 2, 1), (1, 0, 3, 1), (1, 1, -2, 1), (0, 0, -1, 0),
+    (1, 0, -2, 0), (1, -1, 2, 1), (0, 0, 1, 0), (1, 0, 2, 0), (1, 1, 2, 1), (0, -1, -1, 0), (1, -1, -2, 0),
+    (0, -1, 1, 0), (1, -1, 2, 0), (0, -1, -1, 1), (1, 2, -1, 1), (0, 1, -1, 0), (1, 1, -2, 0), (0, 1, 1, 0),
+    (1, 1, 2, 0), (0, -1, 1, 1), (1, 2, 1, 1), (0, 2, -1, 0), (1, 2, -2, 0), (0, 0, -3, 1), (1, -1, -3, 1),
+    (0, 2, 1, 0), (1, 2, 2, 0), (1, 0, 4, 1), (1, 1, -3, 1), (0, 0, -2, 0), (1, 0, -3, 0), (0, 0, 3, 1),
+    (1, -1, 3, 1), (0, 0, 2, 0), (1, 0, 3, 0), (0, -1, -2, 0), (1, -1, -3, 0), (1, 1, 3, 1), (0, -1, 2, 0),
+    (1, -1, 3, 0), (0, -1, -2, 1), (1, 2, -2, 1), (0, 1, -2, 0), (1, 1, -3, 0), (0, 1, 2, 0), (0, 2, 2, 0),
+    (2, 8, 0, 0), (2, 9, 0, 0), (1, 1, 3, 0), (0, -1, 2, 1), (1, 2, 2, 1), (2, 10, 0, 0), (0, 2, -2, 0),
+    (1, 2, -3, 0), (0, 0, 4, 1), (1, -1, 4, 1), (1, 2, 3, 0), (0, 0, -3, 0), (1, 0, 4, 0), (1, 1, 4, 1),
+    (0, -1, -3, 0), (1, -1, 4, 0), (0, -1, -3, 1), (1, 2, -3, 1), (0, 1, -3, 0), (1, 1, 4, 0), (0, -1, 3, 1),
+    (1, 2, 3, 1), (0, 2, -3, 0), (1, 2, 4, 0), (0, 1, 0, 1), (0, 1, -1, 1), (0, 1, 1, 1), (0, 2, 0, 1),
+    (0, 1, 2, 1), (0, 2, -1, 1), (0, 2, 1, 1), (0, 2, 2, 1), (2, 11, 0, 0), (2, 12, 0, 0), (2, 13, 0, 0),
+    (2, 14, 0, 0), (0, -1, 4, 1), (1, 2, 4, 1), (0, 0, 3, 0), (0, -1, 3, 0), (0, 1, 3, 0), (0, 2, 3, 0),
+    (0, 0, 4, 0), (0, -1, 4, 0), (0, 1, 4, 0), (0, 2, 4, 0), (2, 15, 0, 0), (2, 16, 0, 0), (2, 17, 0, 0),
+    (0, 1, -2, 1), (0, 1, -3, 1), (0, 1, 3, 1), (0, 2, -2, 1), (0, 1, 4, 1), (0, 2, -3, 1), (0, 2, 3, 1),
+    (0, 2, 4, 1), (2, 18, 0, 0), (2, 19, 0, 0), (2, 20, 0, 0), (2, 21, 0, 0),
 )
 
 
@@ -100,13 +97,6 @@
     for peer in peers:
         pl.semaphore_signal(barrier, inc=1, device_id=peer, device_id_type=MESH)
 
-    row = lax.broadcasted_iota(jnp.int32, (ROWS, 128), 0)
-    live = jnp.zeros((ROWS, 128), F32)
-    for r in range(ROWS):
-        live = jnp.where(row == r, mask_ref[r].astype(F32), live)
-    x[0:ROWS, MASK_AT:WIDE] = live.astype(BF16)
-    cot_copy.wait()
-    x[0:ROWS, D:MASK_AT] = (cot[...].astype(F32) * live[:, 0:1]).astype(BF16)
     tok_copy.wait()
     pl.semaphore_wait(barrier, len(peers))
 
@@ -129,6 +119,18 @@
             device_id_type=MESH,
         )
 
+    for dst in ((-1, 0, 0), (1, 0, 0), (0, -1, 0), (0, 1, 0)):
+        hop(*dst).start()
+    row = lax.broadcasted_iota(jnp.int32, (ROWS, 128), 0)
+    live = jnp.zeros((ROWS, 128), F32)
+    for r in range(ROWS):
+        live = jnp.where(row == r, mask_ref[r].astype(F32), live)
+    x[0:ROWS, MASK_AT:WIDE] = live.astype(BF16)
+    cot_copy.wait()
+    x[0:ROWS, D:MASK_AT] = (cot[...].astype(F32) * live[:, 0:1]).astype(BF16)
+    for dst in ((0, -1, 1), (0, 1, 1), (-1, 0, 1), (1, 0, 1)):
+        hop(*dst).start()
+
     wg_copy.start()
     wu_copy.start()
     wd_copy.start()
@@ -157,7 +159,7 @@
         def run():
             if copy is not None:
                 copy.wait()
-            part = lax.dot_general(x[tokens_of(c), cols], w[:, cols], NT, preferred_element_type=F32)
+            part = lax.dot_general(w[:, cols], x[tokens_of(c), cols], NT, preferred_element_type=F32)
             if cols.start == 0:
                 out[...] = part
             else:
@@ -169,17 +171,17 @@
         def run():
             if c == 0:
                 wd_copy.wait()
-            back = lax.dot_general(x[tokens_of(c), D:MASK_AT], wd[...], NT, preferred_element_type=F32)
+            back = lax.dot_general(wd[...], x[tokens_of(c), D:MASK_AT], NT, preferred_element_type=F32)
             operand = back * up[...] * curvature(gate[...]) * tan[...]
-            op[tokens_of(c), :] = operand.astype(BF16)
+            op[:, tokens_of(c)] = operand.astype(BF16)
 
         return run
 
     work = [make_signs(k) for k in range(8)]
     for c in range(N_CHUNK):
-        for cols in (slice(0, D),) if c < N_CHUNK - 1 else (slice(0, SPLIT), slice(SPLIT, D)):
-            work.append(make_dot(c, gate, wg, wg_copy if c == 0 else None, cols))
-            work.append(make_dot(c, up, wu, wu_copy if c == 0 else None, cols))
+        for cols in (slice(0, SPLIT), slice(SPLIT, D)):
+            work.append(make_dot(c, gate, wg, wg_copy if c == cols.start == 0 else None, cols))
+            work.append(make_dot(c, up, wu, wu_copy if c == cols.start == 0 else None, cols))
             work.append(make_dot(c, tan, sign, None, cols))
         work.append(make_op(c))
     for what, dy, dz, fam in PLAN:
@@ -231,7 +233,7 @@
     def product(k, of_core):
         start = (lax.rem(xi + k, NX) * 2 + of_core) * OUT_ROWS
         cols = pl.ds(pl.multiple_of(start, OUT_ROWS), OUT_ROWS)
-        return lax.dot_general(op[...], x[:, cols], TN, preferred_element_type=F32)
+        return jnp.dot(op[...], x[:, cols], preferred_element_type=F32)
 
     for k in (2, 1, 3, 0):
         core_out[k] = product(k, 1 - core).astype(BF16)
@@ -272,17 +274,21 @@
         count_copy(1, d, at_x(1)).wait_recv()
     total = pair + cnt_in[1] + cnt_in[2] + cnt_in[3]
     live_count = total[0:1, 0:1]
+    own_cols = pl.ds(pl.multiple_of(dp * OUT_ROWS, OUT_ROWS), OUT_ROWS)
     x_copy(1, 1, 0, at_x(1)).wait_recv()
+    own[0, HALF:WIDTH] += x_in[0, HALF:WIDTH].astype(F32)
     x_copy(3, 0, 2, at_x(-1)).wait_recv()
+    own[0, 0:HALF] += x_in[2, 0:HALF].astype(F32)
     x_copy(1, 0, 0, at_x(1)).wait_recv()
+    hess = own[0, 0:HALF] + x_in[0, 0:HALF].astype(F32)
+    out_ref[0:HALF, :] = sign[0:HALF, own_cols].astype(F32) * (hess / live_count)
     x_copy(3, 1, 2, at_x(-1)).wait_recv()
-    hess = own[0] + x_in[0].astype(F32) + x_in[2].astype(F32)
-    own_signs = sign[:, pl.ds(pl.multiple_of(dp * OUT_ROWS, OUT_ROWS), OUT_ROWS)].astype(F32)
-    out_ref[...] = own_signs * (hess / live_count)
-
-    for what, dy, dz, fam in PLAN:
-        if what == 1:
-            hop(dy, dz, fam).wait_send()
+    hess = own[0, HALF:WIDTH] + x_in[2, HALF:WIDTH].astype(F32)
+    out_ref[HALF:WIDTH, :] = sign[HALF:WIDTH, own_cols].astype(F32) * (hess / live_count)
+
+    for at in range(1, NY * NZ):
+        for fam in (0, 1):
+            hop(DY[at % 4], DZ[at // 4], fam).wait_send()
     for k in range(4):
         core_copy(k).wait_send()
     for k in (1, 2, 3):
@@ -309,10 +315,10 @@
             vmem((WIDTH, D), BF16),
             vmem((WIDTH, D), BF16),
             vmem((WIDTH, D), BF16),
-            vmem((CHUNK, WIDTH), F32),
-            vmem((CHUNK, WIDTH), F32),
-            vmem((CHUNK, WIDTH), F32),
-            vmem((N_CHUNK * CHUNK, WIDTH), BF16),
+            vmem((WIDTH, CHUNK), F32),
+            vmem((WIDTH, CHUNK), F32),
+            vmem((WIDTH, CHUNK), F32),
+            vmem((WIDTH, N_CHUNK * CHUNK), BF16),
             vmem((4, WIDTH, OUT_ROWS), F32),
             vmem((4, WIDTH, OUT_ROWS), BF16),
             vmem((4, WIDTH, OUT_ROWS), BF16),

time: 93 us -> 88.5 us (0.952)
  Pallas kernels: 90 us -> 85.5 us
    pallas_call x1, Pallas kernels: 90 us -> 85.5 us  [per_device(): pl.pallas_call(kernel, out_shape=jax.ShapeDtypeStruct((WIDTH, OUT_ROWS),...]
where the time goes in v3:
time: 88.5 us; the launch traced here: 88.3 us
  Pallas kernels  85.5 us (97%)
  local copies, waits for them, and re-layouts  2.16 us (2%)
    pallas_call x1, Pallas kernels, per_device(): pl.pallas_call(kernel, out_shape=jax.ShapeDtypeStruct((WIDTH, OUT_ROWS),...  85.5 us
    unnamed x1, local copies, waits for them, and re-layouts  2.16 us

profile of v3, /device:TPU:1, one launch (start us, length us, event | category | flops | bytes accessed | tf_op | source)
XLA Modules:
  0.0 88.3 jit_solution(11002711222925812813)
XLA Ops:
  0.7 85.5 %shard_map.73 = f32[448,512]{1,0:T(8,128)} custom-call(bf16[16,4096]{1,0:T(8,128)(2,1)} %tok_ref.1, bf16[16,4096]{1,0:T(8,128)(2,1)} %cot_ref.1, s32[16]{0:T(128)} %mask_ref.1, s32[1]{0:T(128)S(6)} %copy.9.seed_ref, bf16[448,4096]{1,0:T(8,128)(2,1)} %bitcast.4, bf16[448,4096]{1,0:T(8,128)(2,1)} %bitcast.5, bf16[448,4096]{1,0:T(8,128)(2,1)} %wd_hbm.1), custom_call_target="tpu_custom_call" | custom-call | flops 9400000512 | bytes 12000000 | tf_op jit(solution)/shard_map/pallas_call | solution.py:306
  86.2 2.2 %copy.10 = f32[512,448]{0,1:T(8,128)} copy(f32[512,448]{0,1:T(8,128)} %bitcast.3) | data formatting | bytes 1835008

commit v4 on v3

--- a/solution.py
+++ b/solution.py
@@ -192,6 +192,63 @@
         else:
             work[dy]()
 
+    def core_copy(k, part=None):
+        rows = pl.ds(0, WIDTH) if part is None else rows_of(part)
+        sem = k if part is None else 4 + part
+        return pltpu.make_async_remote_copy(
+            src_ref=core_out.at[k, rows],
+            dst_ref=core_in.at[k, rows],
+            send_sem=core_send.at[sem],
+            recv_sem=core_recv.at[sem],
+            device_id=partner,
+            device_id_type=MESH,
+        )
+
+    def rows_of(half):
+        return pl.ds(half * HALF, HALF)
+
+    def x_copy(k, half, dst, device):
+        return pltpu.make_async_remote_copy(
+            src_ref=x_out.at[k - 1, rows_of(half)],
+            dst_ref=x_in.at[dst, rows_of(half)],
+            send_sem=x_send.at[k - 1, half],
+            recv_sem=x_recv.at[dst, half],
+            device_id=device,
+            device_id_type=MESH,
+        )
+
+    def product(k, of_core, rows=slice(0, WIDTH)):
+        start = (lax.rem(xi + k, NX) * 2 + of_core) * OUT_ROWS
+        cols = pl.ds(pl.multiple_of(start, OUT_ROWS), OUT_ROWS)
+        return jnp.dot(op[rows, :], x[:, cols], preferred_element_type=F32)
+
+    halves = (slice(0, HALF), slice(HALF, WIDTH))
+    for part in (0, 1):
+        core_out[2, halves[part]] = product(2, 1 - core, halves[part]).astype(BF16)
+        core_copy(2, part).start()
+    own[2] = product(2, core)
+    core_out[1] = product(1, 1 - core).astype(BF16)
+    core_copy(1).start()
+    for part, device in ((0, at_x(1)), (1, at_x(-1))):
+        core_copy(2, part).wait_recv()
+        x_out[1, halves[part]] = (own[2, halves[part]] + core_in[2, halves[part]].astype(F32)).astype(BF16)
+        x_copy(2, part, 1, device).start()
+    own[1] = product(1, core)
+    core_out[3] = product(3, 1 - core).astype(BF16)
+    core_copy(3).start()
+    core_copy(1).wait_recv()
+    own[1] += core_in[1].astype(F32)
+    x_out[0, HALF:WIDTH] = own[1, HALF:WIDTH].astype(BF16)
+    x_copy(1, 1, 0, at_x(1)).start()
+    own[3] = product(3, core)
+    core_out[0] = product(0, 1 - core).astype(BF16)
+    core_copy(0).start()
+    core_copy(3).wait_recv()
+    own[3] += core_in[3].astype(F32)
+    x_out[2, 0:HALF] = own[3, 0:HALF].astype(BF16)
+    x_copy(3, 0, 2, at_x(-1)).start()
+    own[0] = product(0, core)
+
     count = jnp.sum(x[:, MASK_AT:WIDE].astype(F32), axis=0, keepdims=True)
     cnt_out[0] = jnp.broadcast_to(count, (8, 128))
 
@@ -207,53 +264,6 @@
 
     count_copy(0, 0, partner).start()
 
-    def core_copy(k):
-        return pltpu.make_async_remote_copy(
-            src_ref=core_out.at[k],
-            dst_ref=core_in.at[k],
-            send_sem=core_send.at[k],
-            recv_sem=core_recv.at[k],
-            device_id=partner,
-            device_id_type=MESH,
-        )
-
-    def rows_of(half):
-        return pl.ds(half * HALF, HALF)
-
-    def x_copy(k, half, dst, device):
-        return pltpu.make_async_remote_copy(
-            src_ref=x_out.at[k - 1, rows_of(half)],
-            dst_ref=x_in.at[dst, rows_of(half)],
-            send_sem=x_send.at[k - 1, half],
-            recv_sem=x_recv.at[dst, half],
-            device_id=device,
-            device_id_type=MESH,
-        )
-
-    def product(k, of_core):
-        start = (lax.rem(xi + k, NX) * 2 + of_core) * OUT_ROWS
-        cols = pl.ds(pl.multiple_of(start, OUT_ROWS), OUT_ROWS)
-        return jnp.dot(op[...], x[:, cols], preferred_element_type=F32)
-
-    for k in (2, 1, 3, 0):
-        core_out[k] = product(k, 1 - core).astype(BF16)
-        core_copy(k).start()
-        own[k] = product(k, core)
-        if k == 2:
-            continue
-        last = {1: 2, 3: 1, 0: 3}[k]
-        core_copy(last).wait_recv()
-        own[last] += core_in[last].astype(F32)
-        if last == 2:
-            x_out[1] = own[2].astype(BF16)
-            x_copy(2, 0, 1, at_x(1)).start()
-            x_copy(2, 1, 1, at_x(-1)).start()
-        elif last == 1:
-            x_out[0, HALF:WIDTH] = own[1, HALF:WIDTH].astype(BF16)
-            x_copy(1, 1, 0, at_x(1)).start()
-        elif last == 3:
-            x_out[2, 0:HALF] = own[3, 0:HALF].astype(BF16)
-            x_copy(3, 0, 2, at_x(-1)).start()
     count_copy(0, 0, partner).wait_recv()
     pair = cnt_out[0] + cnt_in[0]
     cnt_out[1] = pair
@@ -289,8 +299,10 @@
     for at in range(1, NY * NZ):
         for fam in (0, 1):
             hop(DY[at % 4], DZ[at // 4], fam).wait_send()
-    for k in range(4):
+    for k in (0, 1, 3):
         core_copy(k).wait_send()
+    for part in (0, 1):
+        core_copy(2, part).wait_send()
     for k in (1, 2, 3):
         for half in (0, 1):
             x_copy(k, half, 0, at_x(1)).wait_send()
@@ -329,8 +341,8 @@
             dma((5,)),
             dma((2, NY * NZ)),
             dma((2, NY * NZ)),
-            dma((4,)),
-            dma((4,)),
+            dma((6,)),
+            dma((6,)),
             dma((3, 2)),
             dma((3, 2)),
             dma((4,)),

time: 88.5 us -> 87.9 us (level)
  no operation moved by 1% of the time
where the time goes in v4:
time: 87.9 us; the launch traced here: 87.8 us
  Pallas kernels  85 us (97%)
  local copies, waits for them, and re-layouts  2.16 us (2%)
    pallas_call x1, Pallas kernels, per_device(): pl.pallas_call(kernel, out_shape=jax.ShapeDtypeStruct((WIDTH, OUT_ROWS),...  85 us
    unnamed x1, local copies, waits for them, and re-layouts  2.16 us

profile of v4, /device:TPU:1, one launch (start us, length us, event | category | flops | bytes accessed | tf_op | source)
XLA Modules:
  0.0 87.8 jit_solution(7524087119380479003)
XLA Ops:
  0.7 85.0 %shard_map.73 = f32[448,512]{1,0:T(8,128)} custom-call(bf16[16,4096]{1,0:T(8,128)(2,1)} %tok_ref.1, bf16[16,4096]{1,0:T(8,128)(2,1)} %cot_ref.1, s32[16]{0:T(128)} %mask_ref.1, s32[1]{0:T(128)S(6)} %copy.9.seed_ref, bf16[448,4096]{1,0:T(8,128)(2,1)} %bitcast.4, bf16[448,4096]{1,0:T(8,128)(2,1)} %bitcast.5, bf16[448,4096]{1,0:T(8,128)(2,1)} %wd_hbm.1), custom_call_target="tpu_custom_call" | custom-call | flops 9400000512 | bytes 12000000 | tf_op jit(solution)/shard_map/pallas_call | solution.py:318
  85.6 2.2 %copy.10 = f32[512,448]{0,1:T(8,128)} copy(f32[512,448]{0,1:T(8,128)} %bitcast.3) | data formatting | bytes 1835008

commit v5 on v4

--- a/solution.py
+++ b/solution.py
@@ -32,8 +32,8 @@
 
 PLAN = (
     (2, 0, 0, 0), (2, 1, 0, 0), (2, 2, 0, 0), (2, 3, 0, 0), (2, 4, 0, 0), (2, 5, 0, 0), (2, 6, 0, 0),
-    (2, 7, 0, 0), (0, -1, 0, 0), (1, 2, 0, 0), (0, 0, -1, 1), (1, 0, -2, 1), (1, -1, -1, 1), (1, 1, -1, 1),
-    (1, -1, -1, 0), (1, -1, 1, 0), (0, 0, 1, 1), (1, 0, 2, 1), (1, -1, 1, 1), (0, 1, 0, 0), (1, 1, -1, 0),
+    (2, 7, 0, 0), (0, -1, 0, 0), (1, 2, 0, 0), (1, -1, -1, 0), (0, 0, -1, 1), (1, 0, -2, 1), (1, -1, -1, 1),
+    (1, 1, -1, 1), (1, -1, 1, 0), (0, 1, 0, 0), (1, 1, -1, 0), (0, 0, 1, 1), (1, 0, 2, 1), (1, -1, 1, 1),
     (1, 1, 1, 1), (1, 1, 1, 0), (0, 2, 0, 0), (1, 2, -1, 0), (0, -1, 0, 1), (1, 2, 0, 1), (1, 2, 1, 0),
     (0, 0, -2, 1), (1, 0, -3, 1), (1, -1, -2, 1), (0, 0, 2, 1), (1, 0, 3, 1), (1, 1, -2, 1), (0, 0, -1, 0),
     (1, 0, -2, 0), (1, -1, 2, 1), (0, 0, 1, 0), (1, 0, 2, 0), (1, 1, 2, 1), (0, -1, -1, 0), (1, -1, -2, 0),
@@ -41,13 +41,13 @@
     (1, 1, 2, 0), (0, -1, 1, 1), (1, 2, 1, 1), (0, 2, -1, 0), (1, 2, -2, 0), (0, 0, -3, 1), (1, -1, -3, 1),
     (0, 2, 1, 0), (1, 2, 2, 0), (1, 0, 4, 1), (1, 1, -3, 1), (0, 0, -2, 0), (1, 0, -3, 0), (0, 0, 3, 1),
     (1, -1, 3, 1), (0, 0, 2, 0), (1, 0, 3, 0), (0, -1, -2, 0), (1, -1, -3, 0), (1, 1, 3, 1), (0, -1, 2, 0),
-    (1, -1, 3, 0), (0, -1, -2, 1), (1, 2, -2, 1), (0, 1, -2, 0), (1, 1, -3, 0), (0, 1, 2, 0), (0, 2, 2, 0),
-    (2, 8, 0, 0), (2, 9, 0, 0), (1, 1, 3, 0), (0, -1, 2, 1), (1, 2, 2, 1), (2, 10, 0, 0), (0, 2, -2, 0),
-    (1, 2, -3, 0), (0, 0, 4, 1), (1, -1, 4, 1), (1, 2, 3, 0), (0, 0, -3, 0), (1, 0, 4, 0), (1, 1, 4, 1),
+    (1, -1, 3, 0), (0, -1, -2, 1), (1, 2, -2, 1), (0, 1, -2, 0), (1, 1, -3, 0), (0, 1, 2, 0), (1, 1, 3, 0),
+    (0, -1, 2, 1), (1, 2, 2, 1), (0, 2, -2, 0), (1, 2, -3, 0), (0, 2, 2, 0), (2, 8, 0, 0), (0, 0, 4, 1),
+    (1, -1, 4, 1), (1, 2, 3, 0), (2, 9, 0, 0), (0, 0, -3, 0), (1, 0, 4, 0), (2, 10, 0, 0), (1, 1, 4, 1),
     (0, -1, -3, 0), (1, -1, 4, 0), (0, -1, -3, 1), (1, 2, -3, 1), (0, 1, -3, 0), (1, 1, 4, 0), (0, -1, 3, 1),
     (1, 2, 3, 1), (0, 2, -3, 0), (1, 2, 4, 0), (0, 1, 0, 1), (0, 1, -1, 1), (0, 1, 1, 1), (0, 2, 0, 1),
     (0, 1, 2, 1), (0, 2, -1, 1), (0, 2, 1, 1), (0, 2, 2, 1), (2, 11, 0, 0), (2, 12, 0, 0), (2, 13, 0, 0),
-    (2, 14, 0, 0), (0, -1, 4, 1), (1, 2, 4, 1), (0, 0, 3, 0), (0, -1, 3, 0), (0, 1, 3, 0), (0, 2, 3, 0),
+    (0, -1, 4, 1), (1, 2, 4, 1), (2, 14, 0, 0), (0, 0, 3, 0), (0, -1, 3, 0), (0, 1, 3, 0), (0, 2, 3, 0),
     (0, 0, 4, 0), (0, -1, 4, 0), (0, 1, 4, 0), (0, 2, 4, 0), (2, 15, 0, 0), (2, 16, 0, 0), (2, 17, 0, 0),
     (0, 1, -2, 1), (0, 1, -3, 1), (0, 1, 3, 1), (0, 2, -2, 1), (0, 1, 4, 1), (0, 2, -3, 1), (0, 2, 3, 1),
     (0, 2, 4, 1), (2, 18, 0, 0), (2, 19, 0, 0), (2, 20, 0, 0), (2, 21, 0, 0),
@@ -60,8 +60,8 @@
 
 
 def kernel(
-    tok_ref, cot_ref, mask_ref, seed_ref, wg_hbm, wu_hbm, wd_hbm, out_ref,
-    x, cot, wg, wu, wd, sign, gate, up, tan, op, own, core_out, core_in, x_out, x_in, cnt_out, cnt_in,
+    tok_ref, cot_ref, mask_hbm, seed_hbm, wg_hbm, wu_hbm, wd_hbm, out_ref,
+    mask_ref, seed_ref, x, cot, wg, wu, wd, sign, gate, up, tan, op, own, core_out, core_in, x_out, x_in, cnt_out, cnt_in,
     local_sem, ag_send, ag_recv, core_send, core_recv, x_send, x_recv, cnt_send, cnt_recv,
 ):
     dp = lax.axis_index("dp")
@@ -89,8 +89,12 @@
     wg_copy = pltpu.make_async_copy(wg_hbm, wg, local_sem.at[2])
     wu_copy = pltpu.make_async_copy(wu_hbm, wu, local_sem.at[3])
     wd_copy = pltpu.make_async_copy(wd_hbm, wd, local_sem.at[4])
+    mask_copy = pltpu.make_async_copy(mask_hbm, mask_ref, local_sem.at[5])
+    seed_copy = pltpu.make_async_copy(seed_hbm, seed_ref, local_sem.at[6])
     tok_copy.start()
     cot_copy.start()
+    mask_copy.start()
+    seed_copy.start()
 
     peers = [at_y(1), at_y(-1), at_z(1), at_z(-1), partner, at_x(1), at_x(-1), at_x(2)]
     barrier = pltpu.get_barrier_semaphore()
@@ -123,6 +127,7 @@
         hop(*dst).start()
     row = lax.broadcasted_iota(jnp.int32, (ROWS, 128), 0)
     live = jnp.zeros((ROWS, 128), F32)
+    mask_copy.wait()
     for r in range(ROWS):
         live = jnp.where(row == r, mask_ref[r].astype(F32), live)
     x[0:ROWS, MASK_AT:WIDE] = live.astype(BF16)
@@ -134,6 +139,7 @@
     wg_copy.start()
     wu_copy.start()
     wd_copy.start()
+    seed_copy.wait()
     first_col = me * WIDTH
     col_term = (lax.broadcasted_iota(jnp.int32, (WIDTH, 1), 0) + first_col) * jnp.int32(-1640531535)
     col_term = col_term + seed_ref[0] * jnp.int32(668265263)
@@ -312,15 +318,16 @@
 
 def per_device(tokens, cotangent, loss_mask, gate_weight, up_weight, down_weight, probe_seed):
     any_space = pl.BlockSpec(memory_space=pl.ANY)
-    smem = pl.BlockSpec(memory_space=pltpu.SMEM)
     vmem = pltpu.VMEM
     dma = pltpu.SemaphoreType.DMA
     out = pl.pallas_call(
         kernel,
         out_shape=jax.ShapeDtypeStruct((WIDTH, OUT_ROWS), F32),
-        in_specs=[any_space, any_space, smem, smem, any_space, any_space, any_space],
+        in_specs=[any_space] * 7,
         out_specs=pl.BlockSpec(memory_space=vmem),
         scratch_shapes=[
+            pltpu.SMEM((ROWS,), jnp.int32),
+            pltpu.SMEM((1,), jnp.int32),
             vmem((NY * NZ * ROWS, WIDE), BF16),
             vmem((ROWS, D), BF16),
             vmem((WIDTH, D), BF16),
@@ -338,7 +345,7 @@
             vmem((3, WIDTH, OUT_ROWS), BF16),
             vmem((2, 8, 128), F32),
             vmem((4, 8, 128), F32),
-            dma((5,)),
+            dma((7,)),
             dma((2, NY * NZ)),
             dma((2, NY * NZ)),
             dma((6,)),

time: 87.9 us -> 85.2 us (0.969)
  Pallas kernels: 85 us -> 82.2 us
    pallas_call x1, Pallas kernels: 85 us -> 82.2 us  [per_device(): pl.pallas_call(kernel, out_shape=jax.ShapeDtypeStruct((WIDTH, OUT_ROWS),...]
where the time goes in v5:
time: 85.2 us; the launch traced here: 85 us
  Pallas kernels  82.2 us (96%)
  local copies, waits for them, and re-layouts  2.16 us (3%)
    pallas_call x1, Pallas kernels, per_device(): pl.pallas_call(kernel, out_shape=jax.ShapeDtypeStruct((WIDTH, OUT_ROWS),...  82.2 us
    unnamed x1, local copies, waits for them, and re-layouts  2.16 us

profile of v5, /device:TPU:1, one launch (start us, length us, event | category | flops | bytes accessed | tf_op | source)
XLA Modules:
  0.0 85.0 jit_solution(3141255596157759067)
XLA Ops:
  0.7 82.2 %shard_map.73 = f32[448,512]{1,0:T(8,128)} custom-call(bf16[16,4096]{1,0:T(8,128)(2,1)} %tok_ref.1, bf16[16,4096]{1,0:T(8,128)(2,1)} %cot_ref.1, s32[16]{0:T(128)} %mask_hbm.1, s32[1]{0:T(128)S(6)} %copy.9.seed_hbm, bf16[448,4096]{1,0:T(8,128)(2,1)} %bitcast.4, bf16[448,4096]{1,0:T(8,128)(2,1)} %bitcast.5, bf16[448,4096]{1,0:T(8,128)(2,1)} %wd_hbm.1), custom_call_target="tpu_custom_call" | custom-call | flops 9400000512 | bytes 12000000 | tf_op jit(solution)/shard_map/pallas_call | solution.py:323
  82.9 2.2 %copy.10 = f32[512,448]{0,1:T(8,128)} copy(f32[512,448]{0,1:T(8,128)} %bitcast.3) | data formatting | bytes 1835008

commit v6 on v5

--- a/solution.py
+++ b/solution.py
@@ -32,9 +32,9 @@
 
 PLAN = (
     (2, 0, 0, 0), (2, 1, 0, 0), (2, 2, 0, 0), (2, 3, 0, 0), (2, 4, 0, 0), (2, 5, 0, 0), (2, 6, 0, 0),
-    (2, 7, 0, 0), (0, -1, 0, 0), (1, 2, 0, 0), (1, -1, -1, 0), (0, 0, -1, 1), (1, 0, -2, 1), (1, -1, -1, 1),
-    (1, 1, -1, 1), (1, -1, 1, 0), (0, 1, 0, 0), (1, 1, -1, 0), (0, 0, 1, 1), (1, 0, 2, 1), (1, -1, 1, 1),
-    (1, 1, 1, 1), (1, 1, 1, 0), (0, 2, 0, 0), (1, 2, -1, 0), (0, -1, 0, 1), (1, 2, 0, 1), (1, 2, 1, 0),
+    (0, -1, 0, 0), (1, 2, 0, 0), (1, -1, -1, 0), (2, 7, 0, 0), (1, -1, 1, 0), (0, 0, -1, 1), (1, 0, -2, 1),
+    (1, -1, -1, 1), (1, 1, -1, 1), (0, 1, 0, 0), (1, 1, -1, 0), (1, 1, 1, 0), (0, 0, 1, 1), (1, 0, 2, 1),
+    (1, -1, 1, 1), (1, 1, 1, 1), (0, 2, 0, 0), (1, 2, -1, 0), (0, -1, 0, 1), (1, 2, 0, 1), (1, 2, 1, 0),
     (0, 0, -2, 1), (1, 0, -3, 1), (1, -1, -2, 1), (0, 0, 2, 1), (1, 0, 3, 1), (1, 1, -2, 1), (0, 0, -1, 0),
     (1, 0, -2, 0), (1, -1, 2, 1), (0, 0, 1, 0), (1, 0, 2, 0), (1, 1, 2, 1), (0, -1, -1, 0), (1, -1, -2, 0),
     (0, -1, 1, 0), (1, -1, 2, 0), (0, -1, -1, 1), (1, 2, -1, 1), (0, 1, -1, 0), (1, 1, -2, 0), (0, 1, 1, 0),
@@ -42,10 +42,10 @@
     (0, 2, 1, 0), (1, 2, 2, 0), (1, 0, 4, 1), (1, 1, -3, 1), (0, 0, -2, 0), (1, 0, -3, 0), (0, 0, 3, 1),
     (1, -1, 3, 1), (0, 0, 2, 0), (1, 0, 3, 0), (0, -1, -2, 0), (1, -1, -3, 0), (1, 1, 3, 1), (0, -1, 2, 0),
     (1, -1, 3, 0), (0, -1, -2, 1), (1, 2, -2, 1), (0, 1, -2, 0), (1, 1, -3, 0), (0, 1, 2, 0), (1, 1, 3, 0),
-    (0, -1, 2, 1), (1, 2, 2, 1), (0, 2, -2, 0), (1, 2, -3, 0), (0, 2, 2, 0), (2, 8, 0, 0), (0, 0, 4, 1),
-    (1, -1, 4, 1), (1, 2, 3, 0), (2, 9, 0, 0), (0, 0, -3, 0), (1, 0, 4, 0), (2, 10, 0, 0), (1, 1, 4, 1),
-    (0, -1, -3, 0), (1, -1, 4, 0), (0, -1, -3, 1), (1, 2, -3, 1), (0, 1, -3, 0), (1, 1, 4, 0), (0, -1, 3, 1),
-    (1, 2, 3, 1), (0, 2, -3, 0), (1, 2, 4, 0), (0, 1, 0, 1), (0, 1, -1, 1), (0, 1, 1, 1), (0, 2, 0, 1),
+    (0, -1, 2, 1), (1, 2, 2, 1), (0, 2, -2, 0), (1, 2, -3, 0), (0, 2, 2, 0), (1, 2, 3, 0), (0, 0, 4, 1),
+    (1, -1, 4, 1), (2, 8, 0, 0), (0, 0, -3, 0), (1, 0, 4, 0), (1, 1, 4, 1), (2, 9, 0, 0), (2, 10, 0, 0),
+    (0, -1, -3, 1), (1, 2, -3, 1), (0, -1, -3, 0), (1, -1, 4, 0), (0, -1, 3, 1), (1, 2, 3, 1), (0, 1, -3, 0),
+    (1, 1, 4, 0), (0, 2, -3, 0), (1, 2, 4, 0), (0, 1, 0, 1), (0, 1, -1, 1), (0, 1, 1, 1), (0, 2, 0, 1),
     (0, 1, 2, 1), (0, 2, -1, 1), (0, 2, 1, 1), (0, 2, 2, 1), (2, 11, 0, 0), (2, 12, 0, 0), (2, 13, 0, 0),
     (0, -1, 4, 1), (1, 2, 4, 1), (2, 14, 0, 0), (0, 0, 3, 0), (0, -1, 3, 0), (0, 1, 3, 0), (0, 2, 3, 0),
     (0, 0, 4, 0), (0, -1, 4, 0), (0, 1, 4, 0), (0, 2, 4, 0), (2, 15, 0, 0), (2, 16, 0, 0), (2, 17, 0, 0),

time: 85.2 us -> 85.1 us (level)
  no operation moved by 1% of the time
where the time goes in v6:
time: 85.1 us; the launch traced here: 85 us
  Pallas kernels  82.1 us (96%)
  local copies, waits for them, and re-layouts  2.16 us (3%)
    pallas_call x1, Pallas kernels, per_device(): pl.pallas_call(kernel, out_shape=jax.ShapeDtypeStruct((WIDTH, OUT_ROWS),...  82.1 us
    unnamed x1, local copies, waits for them, and re-layouts  2.16 us

profile of v6, /device:TPU:1, one launch (start us, length us, event | category | flops | bytes accessed | tf_op | source)
XLA Modules:
  0.0 85.0 jit_solution(11686275967943908263)
XLA Ops:
  0.7 82.1 %shard_map.73 = f32[448,512]{1,0:T(8,128)} custom-call(bf16[16,4096]{1,0:T(8,128)(2,1)} %tok_ref.1, bf16[16,4096]{1,0:T(8,128)(2,1)} %cot_ref.1, s32[16]{0:T(128)} %mask_hbm.1, s32[1]{0:T(128)S(6)} %copy.9.seed_hbm, bf16[448,4096]{1,0:T(8,128)(2,1)} %bitcast.4, bf16[448,4096]{1,0:T(8,128)(2,1)} %bitcast.5, bf16[448,4096]{1,0:T(8,128)(2,1)} %wd_hbm.1), custom_call_target="tpu_custom_call" | custom-call | flops 9400000512 | bytes 12000000 | tf_op jit(solution)/shard_map/pallas_call | solution.py:323
  82.8 2.2 %copy.10 = f32[512,448]{0,1:T(8,128)} copy(f32[512,448]{0,1:T(8,128)} %bitcast.3) | data formatting | bytes 1835008

commit v7 on v5

--- a/solution.py
+++ b/solution.py
@@ -16,7 +16,7 @@
 HALF = WIDTH // 2
 MASK_AT = 2 * D
 WIDE = 2 * D + 128
-SPLIT = 25 * 128
+SPLIT = 26 * 128
 FAM = ((0, SPLIT), (SPLIT, WIDE - SPLIT))
 DZ = (0, 1, -1, 2, -2, 3, -3, 4)
 DY = (0, 1, -1, 2)
@@ -35,18 +35,18 @@
     (2, 7, 0, 0), (0, -1, 0, 0), (1, 2, 0, 0), (1, -1, -1, 0), (0, 0, -1, 1), (1, 0, -2, 1), (1, -1, -1, 1),
     (1, 1, -1, 1), (1, -1, 1, 0), (0, 1, 0, 0), (1, 1, -1, 0), (0, 0, 1, 1), (1, 0, 2, 1), (1, -1, 1, 1),
     (1, 1, 1, 1), (1, 1, 1, 0), (0, 2, 0, 0), (1, 2, -1, 0), (0, -1, 0, 1), (1, 2, 0, 1), (1, 2, 1, 0),
-    (0, 0, -2, 1), (1, 0, -3, 1), (1, -1, -2, 1), (0, 0, 2, 1), (1, 0, 3, 1), (1, 1, -2, 1), (0, 0, -1, 0),
-    (1, 0, -2, 0), (1, -1, 2, 1), (0, 0, 1, 0), (1, 0, 2, 0), (1, 1, 2, 1), (0, -1, -1, 0), (1, -1, -2, 0),
-    (0, -1, 1, 0), (1, -1, 2, 0), (0, -1, -1, 1), (1, 2, -1, 1), (0, 1, -1, 0), (1, 1, -2, 0), (0, 1, 1, 0),
-    (1, 1, 2, 0), (0, -1, 1, 1), (1, 2, 1, 1), (0, 2, -1, 0), (1, 2, -2, 0), (0, 0, -3, 1), (1, -1, -3, 1),
-    (0, 2, 1, 0), (1, 2, 2, 0), (1, 0, 4, 1), (1, 1, -3, 1), (0, 0, -2, 0), (1, 0, -3, 0), (0, 0, 3, 1),
-    (1, -1, 3, 1), (0, 0, 2, 0), (1, 0, 3, 0), (0, -1, -2, 0), (1, -1, -3, 0), (1, 1, 3, 1), (0, -1, 2, 0),
-    (1, -1, 3, 0), (0, -1, -2, 1), (1, 2, -2, 1), (0, 1, -2, 0), (1, 1, -3, 0), (0, 1, 2, 0), (1, 1, 3, 0),
-    (0, -1, 2, 1), (1, 2, 2, 1), (0, 2, -2, 0), (1, 2, -3, 0), (0, 2, 2, 0), (2, 8, 0, 0), (0, 0, 4, 1),
-    (1, -1, 4, 1), (1, 2, 3, 0), (2, 9, 0, 0), (0, 0, -3, 0), (1, 0, 4, 0), (2, 10, 0, 0), (1, 1, 4, 1),
-    (0, -1, -3, 0), (1, -1, 4, 0), (0, -1, -3, 1), (1, 2, -3, 1), (0, 1, -3, 0), (1, 1, 4, 0), (0, -1, 3, 1),
-    (1, 2, 3, 1), (0, 2, -3, 0), (1, 2, 4, 0), (0, 1, 0, 1), (0, 1, -1, 1), (0, 1, 1, 1), (0, 2, 0, 1),
-    (0, 1, 2, 1), (0, 2, -1, 1), (0, 2, 1, 1), (0, 2, 2, 1), (2, 11, 0, 0), (2, 12, 0, 0), (2, 13, 0, 0),
+    (0, 0, -2, 1), (1, -1, -2, 1), (1, 0, -3, 1), (1, 1, -2, 1), (0, 0, 2, 1), (1, 0, 3, 1), (1, -1, 2, 1),
+    (0, 0, -1, 0), (1, 0, -2, 0), (0, 0, 1, 0), (1, 0, 2, 0), (1, 1, 2, 1), (0, -1, -1, 0), (1, -1, -2, 0),
+    (0, -1, -1, 1), (1, 2, -1, 1), (0, -1, 1, 0), (1, -1, 2, 0), (0, 1, -1, 0), (1, 1, -2, 0), (0, -1, 1, 1),
+    (1, 2, 1, 1), (0, 1, 1, 0), (1, 1, 2, 0), (0, 2, -1, 0), (1, 2, -2, 0), (0, 0, -3, 1), (1, -1, -3, 1),
+    (0, 2, 1, 0), (1, 2, 2, 0), (1, 1, -3, 1), (1, 0, 4, 1), (0, 0, 3, 1), (1, -1, 3, 1), (0, 0, -2, 0),
+    (1, 0, -3, 0), (0, 0, 2, 0), (1, 0, 3, 0), (1, 1, 3, 1), (0, -1, -2, 0), (1, -1, -3, 0), (0, -1, -2, 1),
+    (1, 2, -2, 1), (0, -1, 2, 0), (1, -1, 3, 0), (0, 1, -2, 0), (1, 1, -3, 0), (0, -1, 2, 1), (1, 2, 2, 1),
+    (0, 1, 2, 0), (1, 1, 3, 0), (0, 2, -2, 0), (1, 2, -3, 0), (0, 0, 4, 1), (1, -1, 4, 1), (0, 2, 2, 0),
+    (2, 8, 0, 0), (1, 2, 3, 0), (1, 1, 4, 1), (2, 9, 0, 0), (0, 0, -3, 0), (1, 0, 4, 0), (2, 10, 0, 0),
+    (0, -1, -3, 1), (1, 2, -3, 1), (0, -1, -3, 0), (1, -1, 4, 0), (0, -1, 3, 1), (1, 2, 3, 1), (0, 1, -3, 0),
+    (1, 1, 4, 0), (0, 1, 0, 1), (0, 1, -1, 1), (0, 1, 1, 1), (0, 2, 0, 1), (0, 1, 2, 1), (0, 2, -1, 1),
+    (0, 2, 1, 1), (0, 2, 2, 1), (2, 11, 0, 0), (2, 12, 0, 0), (2, 13, 0, 0), (0, 2, -3, 0), (1, 2, 4, 0),
     (0, -1, 4, 1), (1, 2, 4, 1), (2, 14, 0, 0), (0, 0, 3, 0), (0, -1, 3, 0), (0, 1, 3, 0), (0, 2, 3, 0),
     (0, 0, 4, 0), (0, -1, 4, 0), (0, 1, 4, 0), (0, 2, 4, 0), (2, 15, 0, 0), (2, 16, 0, 0), (2, 17, 0, 0),
     (0, 1, -2, 1), (0, 1, -3, 1), (0, 1, 3, 1), (0, 2, -2, 1), (0, 1, 4, 1), (0, 2, -3, 1), (0, 2, 3, 1),

time: 85.2 us -> 86 us (level)
  no operation moved by 1% of the time
where the time goes in v7:
time: 86 us; the launch traced here: 85.8 us
  Pallas kernels  83 us (97%)
  local copies, waits for them, and re-layouts  2.16 us (3%)
    pallas_call x1, Pallas kernels, per_device(): pl.pallas_call(kernel, out_shape=jax.ShapeDtypeStruct((WIDTH, OUT_ROWS),...  83 us
    unnamed x1, local copies, waits for them, and re-layouts  2.16 us

profile of v7, /device:TPU:1, one launch (start us, length us, event | category | flops | bytes accessed | tf_op | source)
XLA Modules:
  0.0 85.8 jit_solution(6248998898490585170)
XLA Ops:
  0.7 83.0 %shard_map.73 = f32[448,512]{1,0:T(8,128)} custom-call(bf16[16,4096]{1,0:T(8,128)(2,1)} %tok_ref.1, bf16[16,4096]{1,0:T(8,128)(2,1)} %cot_ref.1, s32[16]{0:T(128)} %mask_hbm.1, s32[1]{0:T(128)S(6)} %copy.9.seed_hbm, bf16[448,4096]{1,0:T(8,128)(2,1)} %bitcast.4, bf16[448,4096]{1,0:T(8,128)(2,1)} %bitcast.5, bf16[448,4096]{1,0:T(8,128)(2,1)} %wd_hbm.1), custom_call_target="tpu_custom_call" | custom-call | flops 9400000512 | bytes 12000000 | tf_op jit(solution)/shard_map/pallas_call | solution.py:323
  83.7 2.2 %copy.10 = f32[512,448]{0,1:T(8,128)} copy(f32[512,448]{0,1:T(8,128)} %bitcast.3) | data formatting | bytes 1835008
